TPU v7x, 32 devices: a whole 2x2x4 slice. The times are simulated.
32 devices in a mesh: lat: 4 (over y, x), tm: 8 (over z, core).
Axes of the slice: x: 2, y: 2, z: 4, core: 2. Of those that a mesh axis runs over, the one named last changes fastest.
Arguments:
- light_field: float32 [2, 1024, 2048], P(None, 'lat', 'tm'), may hold values from -6 to 6
- lateral_phase: float32 [1024], replicated, may hold values from -3.140625 to 3.140625
- spectral_phase: float32 [2048], replicated, may hold values from -3.140625 to 3.140625
- occupation: float32 [128, 1024], P(None, 'lat'), may hold values from -0.5 to 1
- bin_decay: float32 [32], replicated, may hold values from 2e-05 to 0.05
- bin_detune: float32 [32], replicated, may hold values from -0.3 to 0.3
- group_bin: int32 [128], replicated, may hold values from 0 to 31
Outputs:
- output_field: float32 [2, 1024, 2048], P(None, 'lat', 'tm')
All inputs are finite; a program needn't handle non-finite values.
Results may differ from a plain program's by a relative error of at most 0.0003.
Values sent between devices are 32-bit elements; how exact they have to be, the bound alone decides.
A program may use at most 128 MiB of HBM per device.

v0:
```python
import math

import jax
import jax.numpy as jnp
from jax import lax
from jax.sharding import PartitionSpec as P

STRETCH = 128
STEPS = 2


GAIN_SCALE = 0.5


def carried_in(value, axis, join, neutral):
    count, mine = (lax.axis_size(axis), lax.axis_index(axis))
    pieces = jax.tree.map(lambda part: lax.all_gather(part, axis), value)
    so_far = jax.tree.map(
        lambda part, zero: jnp.full_like(part, 0) + jnp.asarray(zero, part.dtype), value, neutral
    )

    def lap(position, so_far):
        longer = join(so_far, jax.tree.map(lambda part: part[position], pieces))
        return jax.tree.map(lambda new, old: jnp.where(position < mine, new, old), longer, so_far)

    return lax.fori_loop(0, count - 1, lap, so_far)


def complex_einsum(form, left, right):
    exact = lax.Precision.HIGHEST
    real_part = jnp.einsum(form, left[0], right[0], precision=exact) - jnp.einsum(
        form, left[1], right[1], precision=exact
    )
    imag_part = jnp.einsum(form, left[0], right[1], precision=exact) + jnp.einsum(
        form, left[1], right[0], precision=exact
    )
    return (real_part, imag_part)


def complex_times(left, right):
    return (left[0] * right[0] - left[1] * right[1], left[0] * right[1] + left[1] * right[0])


def angle_table(height, breadth, modulus, sign):
    first = jnp.arange(height, dtype=jnp.int32)[:, None]
    second = jnp.arange(breadth, dtype=jnp.int32)[None, :]
    turns = (first * second % modulus).astype(jnp.float32) * (2.0 * math.pi / modulus)
    return (jnp.cos(turns), sign * jnp.sin(turns))


def time_forward(grid, small_table, twiddle, long_table):
    mixed = complex_einsum("ka,rab->rkb", small_table, grid)
    mixed = complex_times(mixed, twiddle)
    return complex_einsum("rkb,bq->rkq", mixed, long_table)


def time_inverse(spectrum, small_table, twiddle, long_table, length):
    mixed = complex_einsum("rkq,qb->rkb", spectrum, long_table)
    mixed = complex_times(mixed, twiddle)
    result = complex_einsum("ak,rkb->rab", small_table, mixed)
    return (result[0] / length, result[1] / length)


def powers(decay_rate, detuning, exponent):
    magnitude = jnp.exp(-decay_rate * exponent)
    phase_angle = detuning * exponent
    return (magnitude * jnp.cos(phase_angle), -magnitude * jnp.sin(phase_angle))


def on_device(
    light_field, lateral_phase, spectral_phase, occupation, bin_decay, bin_detune, group_bin
):
    lat_count = lax.axis_size("lat")
    time_count = lax.axis_size("tm")
    height = light_field.shape[1]
    span = light_field.shape[2]
    lateral_total = height * lat_count
    time_total = span * time_count
    groups = occupation.shape[0]
    slab = height // time_count
    narrow = span // lat_count
    exact = lax.Precision.HIGHEST
    lat_forward = angle_table(lateral_total, lateral_total, lateral_total, -1.0)
    lat_backward = angle_table(lateral_total, lateral_total, lateral_total, 1.0)
    lateral_turn = (jnp.cos(lateral_phase)[:, None], jnp.sin(lateral_phase)[:, None])
    small_back = angle_table(time_count, time_count, time_count, 1.0)
    twiddle_back = angle_table(time_count, span, time_total, 1.0)
    long_back = angle_table(span, span, span, 1.0)
    spectral_grid = spectral_phase.reshape(span, time_count).T
    spectral_turn = (jnp.cos(spectral_grid), jnp.sin(spectral_grid))
    bins = jnp.arange(bin_decay.shape[0], dtype=jnp.int32)
    onehot = (group_bin[:, None] == bins[None, :]).astype(jnp.float32)
    decay_rate = jnp.dot(onehot, bin_decay, precision=exact)
    detuning = jnp.dot(onehot, bin_detune, precision=exact)
    coupling = jnp.sqrt(-jnp.expm1(-2.0 * decay_rate))[:, None] * occupation
    lags = jnp.arange(STRETCH + 1, dtype=jnp.float32)[:, None]
    lag_powers = powers(decay_rate, detuning, lags)
    lag_grid = (
        jnp.arange(STRETCH, dtype=jnp.int32)[:, None]
        - jnp.arange(STRETCH, dtype=jnp.int32)[None, :]
    )
    inside = (lag_grid >= 0)[None]
    clipped = jnp.maximum(lag_grid, 0)
    leading = (lag_powers[0][1:].T, lag_powers[1][1:].T)
    trailing = (lag_powers[0][:STRETCH][::-1], lag_powers[1][:STRETCH][::-1])
    stretch_step = (lag_powers[0][STRETCH][:, None], lag_powers[1][STRETCH][:, None])
    device_step = powers(decay_rate, detuning, jnp.float32(span))
    weight = GAIN_SCALE / math.sqrt(groups)
    small_forward = angle_table(time_count, time_count, time_count, -1.0)
    twiddle_forward = angle_table(time_count, span, time_total, -1.0)
    long_forward = angle_table(span, span, span, -1.0)
    current = light_field
    block_toeplitz = (
        jnp.where(
            inside,
            jnp.take(
                jnp.dot(coupling.T, lag_powers[0][:STRETCH].T, precision=exact), clipped, axis=1
            ),
            0.0,
        ),
        jnp.where(
            inside,
            jnp.take(
                jnp.dot(coupling.T, lag_powers[1][:STRETCH].T, precision=exact), clipped, axis=1
            ),
            0.0,
        ),
    )
    for repeat in range(STEPS):
        diffract_stacked = current.reshape(2, height, lat_count, narrow)
        lateral_block = lax.all_to_all(
            diffract_stacked, "lat", split_axis=2, concat_axis=1, tiled=True
        )
        piece = (lateral_block[0, :, 0, :], lateral_block[1, :, 0, :])
        lateral_spectrum = complex_einsum("kx,xn->kn", lat_forward, piece)
        lateral_spectrum = complex_times(lateral_spectrum, lateral_turn)
        lateral_result = complex_einsum("xk,kn->xn", lat_backward, lateral_spectrum)
        lateral_joined = (
            jnp.stack([lateral_result[0], lateral_result[1]])[:, :, None, :] / lateral_total
        )
        diffract_turned = lax.all_to_all(
            lateral_joined, "lat", split_axis=1, concat_axis=2, tiled=True
        )
        stacked = diffract_turned.reshape(2, height, span).reshape(2, time_count, slab, span)
        rows = lax.all_to_all(stacked, "tm", split_axis=1, concat_axis=3, tiled=True)[:, 0]
        rows_here = rows.shape[1]
        grid = (
            rows[0].reshape(rows_here, time_count, span),
            rows[1].reshape(rows_here, time_count, span),
        )
        spectrum = time_forward(grid, small_forward, twiddle_forward, long_forward)
        spectrum = complex_times(spectrum, spectral_turn)
        result = time_inverse(spectrum, small_back, twiddle_back, long_back, time_total)
        joined = jnp.stack(
            [result[0].reshape(rows_here, time_total), result[1].reshape(rows_here, time_total)]
        )[:, None]
        turned = lax.all_to_all(joined, "tm", split_axis=3, concat_axis=1, tiled=True)
        current = turned.reshape(2, height, span)
        amplify_rows_here = current.shape[1]
        length = current.shape[2]
        count = length // STRETCH
        amplify_grid = (
            current[0].reshape(amplify_rows_here, count, STRETCH),
            current[1].reshape(amplify_rows_here, count, STRETCH),
        )
        direct = complex_einsum("xji,xci->xcj", block_toeplitz, amplify_grid)
        projected = complex_einsum("xci,ig->cgx", amplify_grid, trailing)
        stretch_ends = (coupling[None] * projected[0], coupling[None] * projected[1])

        def chain_step(running, ends):
            moved = complex_times(stretch_step, running)
            return ((moved[0] + ends[0], moved[1] + ends[1]), running)

        zero_state = jnp.zeros((groups, amplify_rows_here), jnp.float32)
        running, chain = lax.scan(chain_step, (zero_state, zero_state), stretch_ends)

        def combine(earlier, later):
            joint = complex_times((earlier[0], earlier[1]), (later[0], later[1]))
            carried = complex_times(
                (later[0][:, None], later[1][:, None]), (earlier[2], earlier[3])
            )
            return (joint[0], joint[1], carried[0] + later[2], carried[1] + later[3])

        identity = (
            jnp.ones((groups,), jnp.float32),
            jnp.zeros((groups,), jnp.float32),
            jnp.zeros_like(running[0]),
            jnp.zeros_like(running[1]),
        )
        prefix = carried_in(
            (device_step[0], device_step[1], running[0], running[1]), "tm", combine, identity
        )
        starts = powers(
            decay_rate, detuning, (jnp.arange(count, dtype=jnp.float32) * STRETCH)[:, None]
        )
        before = complex_times(
            (starts[0][:, :, None], starts[1][:, :, None]), (prefix[2][None], prefix[3][None])
        )
        states = (before[0] + chain[0], before[1] + chain[1])
        delayed = complex_einsum("cgx,gj->xcj", states, leading)
        summed_re = (direct[0] + delayed[0]).reshape(amplify_rows_here, length)
        summed_im = (direct[1] + delayed[1]).reshape(amplify_rows_here, length)
        current = jnp.stack([current[0] - weight * summed_im, current[1] + weight * summed_re])
    return current


def solution(mesh):
    return jax.shard_map(
        on_device,
        mesh=mesh,
        in_specs=(P(None, "lat", "tm"), P(), P(), P(None, "lat"), P(), P(), P()),
        out_specs=P(None, "lat", "tm"),
        check_vma=False,
    )
```

profile of v0, /device:TPU:0, one launch (start us, length us, event | category | flops | bytes accessed | tf_op | source)
XLA Modules:
  0.0 968.3 jit_solution(17391651202592183172)
XLA Ops:
  8.6 5.2 all-to-all-start
  14.6 7.3 all-to-all-done
  22.1 19.8 %fusion.60 = f32[1024,64]{0,1:T(8,128)S(1)} fusion(f32[1024,64]{0,1:T(8,128)S(1)} %bitcast.447), kind=kOutput, calls=%fused_computation.83 | convolution fusion | flops 821035008 | bytes 524288 | tf_op jit(solution)/shard_map/kx,xn->kn/dot_general | solution.py:31
  42.2 19.8 %fusion.58 = f32[1024,64]{0,1:T(8,128)S(1)} fusion(f32[1024,64]{0,1:T(8,128)S(1)} %bitcast.451), kind=kOutput, calls=%fused_computation.81 | convolution fusion | flops 821035008 | bytes 524288 | tf_op jit(solution)/shard_map/kx,xn->kn/dot_general | solution.py:34
  62.0 19.8 %fusion.152 = f32[1024,64]{0,1:T(8,128)S(1)} fusion(f32[1024,64]{0,1:T(8,128)S(1)} %fusion.60, f32[1024,64]{0,1:T(8,128)S(1)} %bitcast.452), kind=kOutput, calls=%fused_computation.167 | convolution fusion | flops 820051968 | bytes 786432 | tf_op jit(solution)/shard_map/kx,xn->kn/dot_general | solution.py:31
  81.8 20.0 %fusion.155 = f32[1024,64]{0,1:T(8,128)S(1)} fusion(f32[1024,64]{0,1:T(8,128)S(1)} %fusion.58, f32[1024,64]{0,1:T(8,128)S(1)} %bitcast.448), kind=kOutput, calls=%fused_computation.168 | convolution fusion | flops 820051968 | bytes 786432 | tf_op jit(solution)/shard_map/kx,xn->kn/dot_general | solution.py:34
  101.7 19.3 %fusion.78 = f32[1024,64]{0,1:T(8,128)S(1)} fusion(f32[1024,64]{0,1:T(8,128)S(1)} %fusion.155, f32[1024,64]{0,1:T(8,128)S(1)} %fusion.152, f32[1024]{0:T(1024)S(1)} %get-tuple-element.607, f32[1024]{0:T(1024)S(1)} %get-tuple-element.606), kind=kOutput, calls=%fused_computation.96 | convolution fusion | flops 820183040 | bytes 794624 | tf_op jit(solution)/shard_map/xk,kn->xn/dot_general | solution.py:31
  121.0 19.7 %fusion.76 = f32[1024,64]{0,1:T(8,128)S(1)} fusion(f32[1024,64]{0,1:T(8,128)S(1)} %fusion.155, f32[1024,64]{0,1:T(8,128)S(1)} %fusion.152, f32[1024]{0:T(1024)S(1)} %get-tuple-element.607, f32[1024]{0:T(1024)S(1)} %get-tuple-element.606), kind=kOutput, calls=%fused_computation.95 | convolution fusion | flops 820183040 | bytes 794624 | tf_op jit(solution)/shard_map/xk,kn->xn/dot_general | solution.py:34
  140.7 19.4 %fusion.131 = f32[1,1024,1,64]{1,3,2,0:T(8,128)S(1)} fusion(f32[1024,64]{0,1:T(8,128)S(1)} %fusion.78, f32[1024,64]{0,1:T(8,128)S(1)} %fusion.155, f32[1024,64]{0,1:T(8,128)S(1)} %fusion.152, f32[1024]{0:T(1024)S(1)} %get-tuple-element.607, f32[1024]{0:T(1024)S(1)} %get-tuple-element.606), kind=kOutput, calls=%fused_computation.160 | convolution fusion | flops 820248576 | bytes 1056768 | tf_op jit(solution)/shard_map/xk,kn->xn/dot_general | solution.py:31
  160.2 19.8 %fusion.137 = f32[1,1024,1,64]{1,3,2,0:T(8,128)S(1)} fusion(f32[1024,64]{0,1:T(8,128)S(1)} %fusion.76, f32[1024,64]{0,1:T(8,128)S(1)} %fusion.155, f32[1024,64]{0,1:T(8,128)S(1)} %fusion.152, f32[1024]{0:T(1024)S(1)} %get-tuple-element.607, f32[1024]{0:T(1024)S(1)} %get-tuple-element.606), kind=kOutput, calls=%fused_computation.162 | convolution fusion | flops 820248576 | bytes 1056768 | tf_op jit(solution)/shard_map/xk,kn->xn/dot_general | solution.py:34
  181.3 4.4 reduce
  187.7 3.5 all-to-all-start.1
  191.6 6.7 all-to-all-done.1
  203.9 5.3 all-to-all-start.2
  210.6 13.6 %all-to-all-done.2 = f32[2,8,32,256]{3,2,0,1:T(8,128)S(1)} async-done(((f32[2,8,32,256]{3,2,0,1:T(8,128)}), f32[2,8,32,256]{3,2,0,1:T(8,128)S(1)}, u32[]{:S(2)}, u32[]{:S(2)}) %all-to-all-start.2) | async-done | bytes 524320 | tf_op jit(solution)/shard_map/all_to_all | solution.py:145
  241.7 4.3 reshape.453
  246.0 3.5 all-to-all-start.3
  250.9 62.1 %gather_fusion = f32[16384,256]{1,0:T(8,128)} fusion(f32[256,128]{0,1:T(8,128)S(1)} %fusion.571, s32[16384]{0:T(1024)S(1)} %bitcast_clamp_fusion), kind=kCustom, calls=%fused_computation.clone | custom fusion | bytes 33619968 | tf_op jit(solution)/shard_map/jit(_take)/gather | solution.py:116
  313.0 18.1 %copy.261 = f32[128,128,256]{1,0,2:T(8,128)} copy(f32[128,128,256]{2,1,0:T(8,128)} %bitcast.411) | data formatting | bytes 33554432 | tf_op jit(solution)/shard_map/jit(_take)/gather | solution.py:116
  331.4 62.0 %gather_fusion.1 = f32[16384,256]{1,0:T(8,128)} fusion(f32[256,128]{0,1:T(8,128)S(1)} %fusion.569, s32[16384]{0:T(1024)S(1)} %bitcast_clamp_fusion), kind=kCustom, calls=%fused_computation.1.clone | custom fusion | bytes 33619968 | tf_op jit(solution)/shard_map/jit(_take)/gather | solution.py:123
  393.3 18.0 %copy.264 = f32[128,128,256]{1,0,2:T(8,128)} copy(f32[128,128,256]{2,1,0:T(8,128)} %bitcast.410) | data formatting | bytes 33554432 | tf_op jit(solution)/shard_map/jit(_take)/gather | solution.py:123
  411.4 12.0 %all-gather.6 = f32[8,1,128]{2,1,0:T(1,128)S(1)} all-gather(f32[1,1,128]{2,1,0:T(1,128)S(1)} %get-tuple-element.611), channel_id=2, replica_groups=mesh['lat'=4,'tm'=8] {'tm'}, dimensions={0}, use_global_device_ids=true | all-gather | bytes 4608 | tf_op jit(solution)/shard_map/all_gather | solution.py:17
  423.4 8.6 all-gather.7
  441.8 28.7 %fusion.11 = f32[256,2,128]{2,1,0:T(2,128)S(1)} fusion(f32[256,2,128]{2,1,0:T(2,128)S(1)} %reshape_squeeze.26, f32[128,128,256]{1,0,2:T(8,128)} %copy.261, pred[128,128]{1,0:T(8,128)(4,1)S(1)} %get-tuple-element.621, pred[128,128]{1,0:T(8,128)(4,1)S(1)} %get-tuple-element.620), kind=kOutput, calls=%fused_computation.31 | convolution fusion | flops 109051904 | bytes 17334272 | tf_op jit(solution)/shard_map/xji,xci->xcj/dot_general | solution.py:34
  470.7 28.7 %fusion.15 = f32[256,2,128]{2,1,0:T(2,128)S(1)} fusion(f32[256,2,128]{2,1,0:T(2,128)S(1)} %reshape_squeeze.27, f32[128,128,256]{1,0,2:T(8,128)} %copy.264, pred[128,128]{1,0:T(8,128)(4,1)S(1)} %get-tuple-element.621, pred[128,128]{1,0:T(8,128)(4,1)S(1)} %get-tuple-element.620), kind=kOutput, calls=%fused_computation.35 | convolution fusion | flops 109051904 | bytes 17334272 | tf_op jit(solution)/shard_map/xji,xci->xcj/dot_general | solution.py:34
  500.2 28.9 %fusion.10 = f32[256,2,128]{2,1,0:T(2,128)S(1)} fusion(f32[256,2,128]{2,1,0:T(2,128)S(1)} %reshape_squeeze.27, f32[128,128,256]{1,0,2:T(8,128)} %copy.261, pred[128,128]{1,0:T(8,128)(4,1)S(1)} %get-tuple-element.621, pred[128,128]{1,0:T(8,128)(4,1)S(1)} %get-tuple-element.620), kind=kOutput, calls=%fused_computation.30 | convolution fusion | flops 109051904 | bytes 17334272 | tf_op jit(solution)/shard_map/xji,xci->xcj/dot_general | solution.py:31
  530.0 28.7 %fusion.14 = f32[256,2,128]{2,1,0:T(2,128)S(1)} fusion(f32[256,2,128]{2,1,0:T(2,128)S(1)} %reshape_squeeze.26, f32[128,128,256]{1,0,2:T(8,128)} %copy.264, pred[128,128]{1,0:T(8,128)(4,1)S(1)} %get-tuple-element.621, pred[128,128]{1,0:T(8,128)(4,1)S(1)} %get-tuple-element.620), kind=kOutput, calls=%fused_computation.34 | convolution fusion | flops 109051904 | bytes 17334272 | tf_op jit(solution)/shard_map/xji,xci->xcj/dot_general | solution.py:31
  559.5 7.9 while.67
  572.7 11.9 %all_to_all.120 = f32[2,256,4,64]{1,3,0,2:T(8,128)S(1)} all-to-all(f32[2,256,4,64]{1,3,0,2:T(8,128)S(1)} %copy.280), channel_id=1, replica_groups=mesh['lat'=4,'tm'=8] {'lat'}, dimensions={2} | all-to-all | bytes 1048576 | tf_op jit(solution)/shard_map/all_to_all | solution.py:131
  584.9 19.8 %fusion.56 = f32[1024,64]{0,1:T(8,128)S(1)} fusion(f32[1024,64]{0,1:T(8,128)S(1)} %bitcast.449), kind=kOutput, calls=%fused_computation.79 | convolution fusion | flops 821035008 | bytes 524288 | tf_op jit(solution)/shard_map/kx,xn->kn/dot_general | solution.py:31
  604.9 19.8 %fusion.54 = f32[1024,64]{0,1:T(8,128)S(1)} fusion(f32[1024,64]{0,1:T(8,128)S(1)} %bitcast.453), kind=kOutput, calls=%fused_computation.77 | convolution fusion | flops 821035008 | bytes 524288 | tf_op jit(solution)/shard_map/kx,xn->kn/dot_general | solution.py:34
  624.8 20.0 %fusion.158 = f32[1024,64]{0,1:T(8,128)S(1)} fusion(f32[1024,64]{0,1:T(8,128)S(1)} %fusion.56, f32[1024,64]{0,1:T(8,128)S(1)} %bitcast.454), kind=kOutput, calls=%fused_computation.169 | convolution fusion | flops 820051968 | bytes 786432 | tf_op jit(solution)/shard_map/kx,xn->kn/dot_general | solution.py:31
  644.8 19.7 %fusion.161 = f32[1024,64]{0,1:T(8,128)S(1)} fusion(f32[1024,64]{0,1:T(8,128)S(1)} %fusion.54, f32[1024,64]{0,1:T(8,128)S(1)} %bitcast.450), kind=kOutput, calls=%fused_computation.170 | convolution fusion | flops 820051968 | bytes 786432 | tf_op jit(solution)/shard_map/kx,xn->kn/dot_general | solution.py:34
  664.5 19.3 %fusion.70 = f32[1024,64]{0,1:T(8,128)S(1)} fusion(f32[1024,64]{0,1:T(8,128)S(1)} %fusion.161, f32[1024,64]{0,1:T(8,128)S(1)} %fusion.158, f32[1024]{0:T(1024)S(1)} %copy-done.27, f32[1024]{0:T(1024)S(1)} %copy-done.25), kind=kOutput, calls=%fused_computation.92 | convolution fusion | flops 820183040 | bytes 794624 | tf_op jit(solution)/shard_map/xk,kn->xn/dot_general | solution.py:31
  683.8 19.7 %fusion.68 = f32[1024,64]{0,1:T(8,128)S(1)} fusion(f32[1024,64]{0,1:T(8,128)S(1)} %fusion.161, f32[1024,64]{0,1:T(8,128)S(1)} %fusion.158, f32[1024]{0:T(1024)S(1)} %copy-done.27, f32[1024]{0:T(1024)S(1)} %copy-done.25), kind=kOutput, calls=%fused_computation.91 | convolution fusion | flops 820183040 | bytes 794624 | tf_op jit(solution)/shard_map/xk,kn->xn/dot_general | solution.py:34
  703.5 19.5 %fusion.143 = f32[1,1024,1,64]{1,3,2,0:T(8,128)S(1)} fusion(f32[1024,64]{0,1:T(8,128)S(1)} %fusion.70, f32[1024,64]{0,1:T(8,128)S(1)} %fusion.161, f32[1024,64]{0,1:T(8,128)S(1)} %fusion.158, f32[1024]{0:T(1024)S(1)} %copy-done.27, f32[1024]{0:T(1024)S(1)} %copy-done.25), kind=kOutput, calls=%fused_computation.164 | convolution fusion | flops 820248576 | bytes 1056768 | tf_op jit(solution)/shard_map/xk,kn->xn/dot_general | solution.py:31
  723.0 19.9 %fusion.149 = f32[1,1024,1,64]{1,3,2,0:T(8,128)S(1)} fusion(f32[1024,64]{0,1:T(8,128)S(1)} %fusion.68, f32[1024,64]{0,1:T(8,128)S(1)} %fusion.161, f32[1024,64]{0,1:T(8,128)S(1)} %fusion.158, f32[1024]{0:T(1024)S(1)} %copy-done.27, f32[1024]{0:T(1024)S(1)} %copy-done.25), kind=kOutput, calls=%fused_computation.166 | convolution fusion | flops 820248576 | bytes 1056768 | tf_op jit(solution)/shard_map/xk,kn->xn/dot_general | solution.py:34
  743.6 4.4 reduce.3
  749.2 10.4 %all_to_all.121 = f32[4,1,32768]{2,1,0:T(1,128)S(1)} all-to-all(f32[4,1,32768]{2,1,0:T(1,128)S(1)} %reshape.455), channel_id=1, replica_groups=mesh['lat'=4,'tm'=8] {'lat'}, dimensions={0} | all-to-all | bytes 1048576 | tf_op jit(solution)/shard_map/all_to_all | solution.py:141
  764.4 18.2 %all_to_all.122 = f32[2,8,32,256]{3,2,0,1:T(8,128)S(1)} all-to-all(f32[2,8,32,256]{3,2,0,1:T(8,128)S(1)} %copy.285), channel_id=1, replica_groups=mesh['lat'=4,'tm'=8] {'tm'}, dimensions={1} | all-to-all | bytes 1048576 | tf_op jit(solution)/shard_map/all_to_all | solution.py:145
  800.0 4.3 reshape.457
  804.3 3.5 all-to-all-start.7
  807.9 15.2 %all-to-all-done.7 = f32[8,1,16384]{2,1,0:T(1,128)S(1)} async-done(((f32[8,1,16384]{2,1,0:T(1,128)}), f32[8,1,16384]{2,1,0:T(1,128)S(1)}, u32[]{:S(2)}, u32[]{:S(2)}) %all-to-all-start.7) | async-done | bytes 524320 | tf_op jit(solution)/shard_map/all_to_all | solution.py:157
  834.2 28.9 %fusion.13 = f32[256,2,128]{2,1,0:T(2,128)S(1)} fusion(f32[256,2,128]{2,1,0:T(2,128)S(1)} %reshape_squeeze.31, f32[128,128,256]{1,0,2:T(8,128)} %copy.264, pred[128,128]{1,0:T(8,128)(4,1)S(1)} %get-tuple-element.621, pred[128,128]{1,0:T(8,128)(4,1)S(1)} %get-tuple-element.620), kind=kOutput, calls=%fused_computation.33 | convolution fusion | flops 109051904 | bytes 17334272 | tf_op jit(solution)/shard_map/xji,xci->xcj/dot_general | solution.py:34
  863.2 28.7 %fusion.9 = f32[256,2,128]{2,1,0:T(2,128)S(1)} fusion(f32[256,2,128]{2,1,0:T(2,128)S(1)} %reshape_squeeze.30, f32[128,128,256]{1,0,2:T(8,128)} %copy.261, pred[128,128]{1,0:T(8,128)(4,1)S(1)} %get-tuple-element.621, pred[128,128]{1,0:T(8,128)(4,1)S(1)} %get-tuple-element.620), kind=kOutput, calls=%fused_computation.29 | convolution fusion | flops 109051904 | bytes 17334272 | tf_op jit(solution)/shard_map/xji,xci->xcj/dot_general | solution.py:34
  892.1 28.9 %fusion.12 = f32[256,2,128]{2,1,0:T(2,128)S(1)} fusion(f32[256,2,128]{2,1,0:T(2,128)S(1)} %reshape_squeeze.30, f32[128,128,256]{1,0,2:T(8,128)} %copy.264, pred[128,128]{1,0:T(8,128)(4,1)S(1)} %get-tuple-element.621, pred[128,128]{1,0:T(8,128)(4,1)S(1)} %get-tuple-element.620), kind=kOutput, calls=%fused_computation.32 | convolution fusion | flops 109051904 | bytes 17334272 | tf_op jit(solution)/shard_map/xji,xci->xcj/dot_general | solution.py:31
  921.2 28.7 %fusion.8 = f32[256,2,128]{2,1,0:T(2,128)S(1)} fusion(f32[256,2,128]{2,1,0:T(2,128)S(1)} %reshape_squeeze.31, f32[128,128,256]{1,0,2:T(8,128)} %copy.261, pred[128,128]{1,0:T(8,128)(4,1)S(1)} %get-tuple-element.621, pred[128,128]{1,0:T(8,128)(4,1)S(1)} %get-tuple-element.620), kind=kOutput, calls=%fused_computation.28 | convolution fusion | flops 109051904 | bytes 17334272 | tf_op jit(solution)/shard_map/xji,xci->xcj/dot_general | solution.py:31
  950.2 7.9 while.69
  (270 shorter events, 105.4 us)
Async XLA Ops:
  6.5 203.0 %copy-start = (f32[32]{0:T(128)S(1)}, f32[32]{0:T(128)}, u32[]{:S(2)}) copy-start(f32[32]{0:T(128)} %param.21) | copy-start | bytes 388
  8.6 13.2 %all-to-all-start = ((f32[2,256,4,64]{1,3,0,2:T(8,128)}), f32[2,256,4,64]{1,3,0,2:T(8,128)S(1)}, u32[]{:S(2)}, u32[]{:S(2)}) async-start(f32[2,256,4,64]{1,3,0,2:T(8,128)} %copy.247), calls=%async_computation | async-start | bytes 1048576 | tf_op jit(solution)/shard_map/all_to_all | solution.py:131
  14.5 145.6 %copy-start.24 = (f32[1024]{0:T(1024)}, f32[1024]{0:T(1024)S(1)}, u32[]{:S(2)}) copy-start(f32[1024]{0:T(1024)S(1)} %get-tuple-element.606) | copy-start | bytes 12292
  14.5 145.6 %copy-start.26 = (f32[1024]{0:T(1024)}, f32[1024]{0:T(1024)S(1)}, u32[]{:S(2)}) copy-start(f32[1024]{0:T(1024)S(1)} %get-tuple-element.607) | copy-start | bytes 12292
  180.0 11.2 %copy-start.28 = (f32[32]{0:T(128)S(1)}, f32[32]{0:T(128)}, u32[]{:S(2)}) copy-start(f32[32]{0:T(128)} %param.22) | copy-start | bytes 388
  180.0 11.2 %copy-start.29 = (s32[128]{0:T(128)S(1)}, s32[128]{0:T(128)}, u32[]{:S(2)}) copy-start(s32[128]{0:T(128)} %param.23) | copy-start | bytes 1540
  180.1 11.4 %copy-start.17 = (f32[2048]{0:T(1024)S(1)}, f32[2048]{0:T(1024)}, u32[]{:S(2)}) copy-start(f32[2048]{0:T(1024)} %param.19) | copy-start | bytes 24580
  187.7 10.6 %all-to-all-start.1 = ((f32[4,1,32768]{2,1,0:T(1,128)}), f32[4,1,32768]{2,1,0:T(1,128)S(1)}, u32[]{:S(2)}, u32[]{:S(2)}) async-start(f32[4,1,32768]{2,1,0:T(1,128)} %reshape.451), calls=%async_computation.1 | async-start | bytes 1048576 | tf_op jit(solution)/shard_map/all_to_all | solution.py:141
  191.2 39.0 %copy-start.22 = (f32[8,256]{1,0:T(8,128)}, f32[8,256]{1,0:T(8,128)S(1)}, u32[]{:S(2)}) copy-start(f32[8,256]{1,0:T(8,128)S(1)} %get-tuple-element.616) | copy-start | bytes 24580
  191.3 47.4 %copy-start.12 = (f32[8,256]{1,0:T(8,128)}, f32[8,256]{1,0:T(8,128)S(1)}, u32[]{:S(2)}) copy-start(f32[8,256]{1,0:T(8,128)S(1)} %get-tuple-element.617) | copy-start | bytes 24580
  200.4 9.8 %copy-start.16 = (f32[128,256]{1,0:T(8,128)S(1)}, f32[128,256]{1,0:T(8,128)}, u32[]{:S(2)}) copy-start(f32[128,256]{1,0:T(8,128)} %param.20) | copy-start | bytes 393220
  203.9 20.3 %all-to-all-start.2 = ((f32[2,8,32,256]{3,2,0,1:T(8,128)}), f32[2,8,32,256]{3,2,0,1:T(8,128)S(1)}, u32[]{:S(2)}, u32[]{:S(2)}) async-start(f32[2,8,32,256]{3,2,0,1:T(8,128)} %copy.252), calls=%async_computation.2 | async-start | bytes 1048576 | tf_op jit(solution)/shard_map/all_to_all | solution.py:145
  209.2 29.4 %copy-start.14 = (f32[8,256]{1,0:T(8,128)}, f32[8,256]{1,0:T(8,128)S(1)}, u32[]{:S(2)}) copy-start(f32[8,256]{1,0:T(8,128)S(1)} %fusion.314) | copy-start | bytes 24580
  209.4 26.6 %copy-start.18 = (f32[8,256]{1,0:T(8,128)}, f32[8,256]{1,0:T(8,128)S(1)}, u32[]{:S(2)}) copy-start(f32[8,256]{1,0:T(8,128)S(1)} %copy.254) | copy-start | bytes 24580
  209.6 26.4 %copy-start.20 = (f32[8,256]{1,0:T(8,128)}, f32[8,256]{1,0:T(8,128)S(1)}, u32[]{:S(2)}) copy-start(f32[8,256]{1,0:T(8,128)S(1)} %copy.255) | copy-start | bytes 24580
  210.2 222.0 %copy-start.6 = (f32[129,128]{1,0:T(8,128)}, f32[129,128]{1,0:T(8,128)S(1)}, u32[]{:S(2)}) copy-start(f32[129,128]{1,0:T(8,128)S(1)} %get-tuple-element.613) | copy-start | bytes 198148
  246.0 186.2 %all-to-all-start.3 = ((f32[8,1,16384]{2,1,0:T(1,128)}), f32[8,1,16384]{2,1,0:T(1,128)S(1)}, u32[]{:S(2)}, u32[]{:S(2)}) async-start(f32[8,1,16384]{2,1,0:T(1,128)} %reshape.453), calls=%async_computation.3 | async-start | bytes 1048576 | tf_op jit(solution)/shard_map/all_to_all | solution.py:157
  249.5 310.1 %all-gather.13.cloned.1.call-start = ((), (), s32[]{:S(2)}) async-start(), calls=%async_computation.8 | async-start | bytes 1179648 | tf_op jit(solution)/shard_map/all_gather | solution.py:17
  435.8 3.1 copy-start.9
  435.9 3.5 copy-start.10
  441.1 0.7 copy-start.2
  441.1 29.4 %copy-start.3 = (f32[128,256]{1,0:T(8,128)}, f32[128,256]{1,0:T(8,128)S(1)}, u32[]{:S(2)}) copy-start(f32[128,256]{1,0:T(8,128)S(1)} %get-tuple-element.387) | copy-start | bytes 393220
  441.7 117.8 %all-gather.15.cloned.1.call-start = ((), (), s32[]{:S(2)}) async-start(), calls=%async_computation.9 | async-start | bytes 1179648 | tf_op jit(solution)/shard_map/all_gather | solution.py:17
  558.7 9.3 copy-start.7
  558.7 10.5 %copy-start.11 = (f32[256,2,128]{0,2,1:T(8,128)S(1)}, f32[256,2,128]{0,2,1:T(8,128)}, u32[]{:S(2)}) copy-start(f32[256,2,128]{0,2,1:T(8,128)} %copy.266) | copy-start | bytes 786436
  567.4 4.5 copy-start.8
  644.7 19.7 %copy-start.25 = (f32[1024]{0:T(1024)S(1)}, f32[1024]{0:T(1024)}, u32[]{:S(2)}) copy-start(f32[1024]{0:T(1024)} %copy-done.24) | copy-start | bytes 12292
  644.8 19.7 %copy-start.27 = (f32[1024]{0:T(1024)S(1)}, f32[1024]{0:T(1024)}, u32[]{:S(2)}) copy-start(f32[1024]{0:T(1024)} %copy-done.26) | copy-start | bytes 12292
  763.7 20.9 %copy-start.13 = (f32[8,256]{1,0:T(8,128)S(1)}, f32[8,256]{1,0:T(8,128)}, u32[]{:S(2)}) copy-start(f32[8,256]{1,0:T(8,128)} %copy-done.12) | copy-start | bytes 24580
  763.7 20.9 %copy-start.23 = (f32[8,256]{1,0:T(8,128)S(1)}, f32[8,256]{1,0:T(8,128)}, u32[]{:S(2)}) copy-start(f32[8,256]{1,0:T(8,128)} %copy-done.22) | copy-start | bytes 24580
  782.8 7.2 copy-start.19
  782.9 7.2 copy-start.21
  787.3 8.5 copy-start.15
  804.3 18.8 %all-to-all-start.7 = ((f32[8,1,16384]{2,1,0:T(1,128)}), f32[8,1,16384]{2,1,0:T(1,128)S(1)}, u32[]{:S(2)}, u32[]{:S(2)}) async-start(f32[8,1,16384]{2,1,0:T(1,128)} %reshape.457), calls=%async_computation.7 | async-start | bytes 1048576 | tf_op jit(solution)/shard_map/all_to_all | solution.py:157
  807.8 142.3 %all-gather.17.cloned.1.call-start = ((), (), s32[]{:S(2)}) async-start(), calls=%async_computation.10 | async-start | bytes 1179648 | tf_op jit(solution)/shard_map/all_gather | solution.py:17
  833.4 0.7 copy-start.4
  833.4 29.6 %copy-start.5 = (f32[128,256]{1,0:T(8,128)}, f32[128,256]{1,0:T(8,128)S(1)}, u32[]{:S(2)}) copy-start(f32[128,256]{1,0:T(8,128)S(1)} %get-tuple-element.393) | copy-start | bytes 393220
  834.1 116.0 %all-gather.19.cloned.1.call-start = ((), (), s32[]{:S(2)}) async-start(), calls=%async_computation.11 | async-start | bytes 1179648 | tf_op jit(solution)/shard_map/all_gather | solution.py:17
  958.1 3.3 copy-start.1
Sparse Core Ops, SparseCore 0:
  441.9 20.5 all-gather.12
  500.4 20.5 all-gather.14
  834.2 19.4 all-gather.16
  892.3 19.4 all-gather.18
where the time goes:
time: 978 us; the launch traced here: 968 us
  matrix products  588 us (60%)
  local copies, waits for them, and re-layouts  205 us (21%)
  blocking collectives  61 us (6%)
  waiting for transfers between devices  42.9 us (4%)
  other arithmetic  35 us (4%)
  starting transfers between devices  21.1 us (2%)
  between operations  15.2 us (2%)
    dot_general x18, matrix products, complex_einsum(): jnp.einsum(form, left[1], right[1], precision=exact)  147 us
    dot_general x18, matrix products, complex_einsum(): jnp.einsum(form, left[1], right[0], precision=exact)  147 us
    dot_general x18, matrix products, complex_einsum(): jnp.einsum(form, left[0], right[0], precision=exact)  146 us
    dot_general x18, matrix products, complex_einsum(): jnp.einsum(form, left[0], right[1], precision=exact)  146 us
    gather x2, local copies, waits for them, and re-layouts, on_device(): jnp.take(jnp.dot(coupling.T, lag_powers[0][:STRETCH].T, precision=exact),...  80.2 us
    gather x2, local copies, waits for them, and re-layouts, on_device(): jnp.take(jnp.dot(coupling.T, lag_powers[1][:STRETCH].T, precision=exact),...  80 us
    unnamed x76, local copies, waits for them, and re-layouts  23.9 us
    all_gather x2, blocking collectives, carried_in(): pieces = jax.tree.map(lambda part: lax.all_gather(part, axis), value)  20.6 us
  transfers between devices with their start and end apart: 9, of which 4 were waited for; matrix products, arithmetic and copies ran while one was open for 41% of the time, Pallas kernels for 0%

commit v1 on v0

--- a/solution.py
+++ b/solution.py
@@ -1,8 +1,12 @@
+import functools
 import math
 
 import jax
 import jax.numpy as jnp
+import numpy as np
 from jax import lax
+from jax.experimental import pallas as pl
+from jax.experimental.pallas import tpu as pltpu
 from jax.sharding import PartitionSpec as P
 
 STRETCH = 128
@@ -204,9 +208,463 @@
     return current
 
 
+LATS, TIMES, SIDE, BIN_COUNT = 4, 8, 256, 32
+TOTAL = LATS * TIMES
+WIDE = LATS * SIDE
+LONG = TIMES * SIDE
+ROWS = SIDE // TIMES
+F32, BF16 = jnp.float32, jnp.bfloat16
+MESH = pl.DeviceIdType.MESH
+
+
+@functools.cache
+def constants():
+    j = np.arange(SIDE)
+    w = np.exp(-2j * np.pi * (np.outer(j, j) % SIDE) / SIDE)
+    big = np.block([[w.real, w.imag], [-w.imag, w.real]]).astype(np.float32)
+    big_hi = big.astype(jnp.bfloat16)
+    big_lo = (big - big_hi.astype(np.float32)).astype(jnp.bfloat16)
+    tw8 = np.exp(-2j * np.pi * np.outer(np.arange(TIMES), j) / LONG)
+    tau = np.exp(-1j * np.pi * np.arange(LONG).reshape(TIMES, SIDE) / LONG)
+    tau2 = np.exp(-1j * np.pi * j / SIDE)[None]
+    rows = np.concatenate([tw8, tau, tau2, np.zeros((7, SIDE))])
+    rows = np.stack([rows.real, rows.imag]).astype(np.float32)
+    tw4 = np.exp(-2j * np.pi * np.outer(j, np.arange(LATS)) / WIDE)
+    cols = np.concatenate([tw4.real, tw4.imag], axis=1).astype(np.float32)
+    return (big_hi, big_lo, rows, cols)
+
+
+def halves(x):
+    hi = x.astype(BF16)
+    return hi, (x - hi.astype(F32)).astype(BF16)
+
+
+def dot(a, b):
+    return jnp.dot(a, b, preferred_element_type=F32)
+
+
+def dot3(a, b):
+    return dot(a[0], b[0]) + dot(a[1], b[0]) + dot(a[0], b[1])
+
+
+def cmul(a, b):
+    return (a[0] * b[0] - a[1] * b[1], a[0] * b[1] + a[1] * b[0])
+
+
+def conj(a):
+    return (a[0], -a[1])
+
+
+def small_fft(items, sign):
+    count = len(items)
+    if count == 1:
+        return items
+    even, odd = small_fft(items[0::2], sign), small_fft(items[1::2], sign)
+    low, high = [], []
+    for k in range(count // 2):
+        re, im = odd[k]
+        if 8 * k == count:
+            r = math.sqrt(0.5)
+            re, im = (re - sign * im) * r, (im + sign * re) * r
+        elif 4 * k == count:
+            re, im = -sign * im, sign * re
+        elif 8 * k == 3 * count:
+            r = math.sqrt(0.5)
+            re, im = (-re - sign * im) * r, (-im + sign * re) * r
+        low.append((even[k][0] + re, even[k][1] + im))
+        high.append((even[k][0] - re, even[k][1] - im))
+    return low + high
+
+
+def lane_iota(shape):
+    return lax.broadcasted_iota(jnp.int32, shape, len(shape) - 1)
+
+
+def roll(x, shift):
+    shift = shift % 128
+    return pltpu.roll(x, shift, axis=x.ndim - 1) if shift else x
+
+
+def pack(re, im):
+    tiles = []
+    first = lane_iota((re.shape[0], 128)) < 64
+    for p in range(re.shape[1] // 128):
+        a, b = re[:, 128 * p : 128 * p + 128], im[:, 128 * p : 128 * p + 128]
+        tiles.append(jnp.where(first, a, roll(b, 64)))
+        tiles.append(jnp.where(first, roll(a, 64), b))
+    return tiles
+
+
+def unpack(tiles):
+    first = lane_iota(tiles[0].shape) < 64
+    re, im = [], []
+    for p in range(0, len(tiles), 2):
+        a, b = tiles[p], tiles[p + 1]
+        re.append(jnp.where(first, a, roll(b, 64)))
+        im.append(jnp.where(first, roll(a, 64), b))
+    return jnp.concatenate(re, axis=1), jnp.concatenate(im, axis=1)
+
+
+def turn(x):
+    first = lane_iota(x.shape) < 64
+    y = roll(x, 64)
+    return jnp.where(first, -y, y)
+
+
+def kernel(
+    lf, latp, specp, occ, dec_ref, det_ref, gb_ref, wh, wl, rows_ref, cols_ref,
+    out,
+    s1, r1, s2, r2, s3, r3, s4, r4,
+    tw_c, tw_s, ph_c, ph_s, ct, q_hi, q_lo, p_hi, p_lo, kev, kod, kfe, kfo, spec,
+    ss1, rs1, ss2, rs2, ss3, rs3, ss4, rs4,
+):
+    l, m = lax.axis_index("lat"), lax.axis_index("tm")
+    me = l * TIMES + m
+    weight = GAIN_SCALE / math.sqrt(occ.shape[0])
+
+    def other(d):
+        t = lax.rem(me + d, TOTAL)
+        return t, t // TIMES, lax.rem(t, TIMES)
+
+    barrier = pltpu.get_barrier_semaphore()
+
+    def greet(d, carry):
+        t, tl, tm = other(d)
+        pl.semaphore_signal(barrier, inc=1, device_id=(tl, tm), device_id_type=MESH)
+        return carry
+
+    lax.fori_loop(1, TOTAL, greet, 0)
+
+    def remote(src, dst, send, recv, tl, tm):
+        return pltpu.make_async_remote_copy(
+            src_ref=src, dst_ref=dst, send_sem=send, recv_sem=recv,
+            device_id=(tl, tm), device_id_type=MESH,
+        )
+
+    def lat_send(s, r, ss, rs, d):
+        t = lax.rem(l + d, LATS)
+        return remote(s.at[t], r.at[l], ss.at[t], rs.at[l], t, m)
+
+    def lat_recv(s, r, ss, rs, d):
+        t = lax.rem(l + d, LATS)
+        return remote(s.at[t], r.at[t], ss.at[t], rs.at[t], t, m)
+
+    def to_rows(d):
+        t, tl, tm = other(d)
+        src = s2.at[tl, pl.ds(pl.multiple_of(tm * ROWS, ROWS), ROWS)]
+        return remote(src, r2.at[m, l], ss2.at[t], rs2.at[me], tl, tm)
+
+    def from_columns(d):
+        t, tl, tm = other(d)
+        return remote(r2.at[tm, tl], r2.at[tm, tl], ss2.at[t], rs2.at[t], tl, tm)
+
+    def to_columns(d):
+        t, tl, tm = other(d)
+        return remote(s3.at[tm, tl], r3.at[l, m], ss3.at[t], rs3.at[me], tl, tm)
+
+    def from_rows(d):
+        t, tl, tm = other(d)
+        return remote(r3.at[tl, tm], r3.at[tl, tm], ss3.at[t], rs3.at[t], tl, tm)
+
+    def each(make, act):
+        def body(d, carry):
+            act(make(d))
+            return carry
+
+        lax.fori_loop(1, TOTAL, body, 0)
+
+    for t, tile in enumerate(pack(lf[0], lf[1])):
+        s1[t] = tile
+    pl.semaphore_wait(barrier, TOTAL - 1)
+    first = [lat_send(s1, r1, ss1, rs1, d) for d in range(1, LATS)]
+    for copy in first:
+        copy.start()
+    r1[l] = s1[l]
+
+    whole = (SIDE, 128)
+    sign = jnp.where(lane_iota(whole) < 64, -1.0, 1.0)
+    phase = latp[...]
+    turn_c, turn_s = jnp.cos(phase) * (1.0 / WIDE), jnp.sin(phase) * (1.0 / WIDE)
+    for k in range(LATS):
+        tw_c[k] = jnp.broadcast_to(cols_ref[:, k : k + 1], whole)
+        tw_s[k] = jnp.broadcast_to(cols_ref[:, LATS + k : LATS + k + 1], whole) * sign
+        ph_c[k] = jnp.broadcast_to(turn_c[:, k : k + 1], whole)
+        ph_s[k] = jnp.broadcast_to(turn_s[:, k : k + 1], whole) * sign
+    spec[0] = jnp.cos(specp[...]) * (1.0 / LONG)
+    spec[1] = jnp.sin(specp[...]) * (1.0 / LONG)
+
+    dec_row, det_row = dec_ref[...], det_ref[...]
+    square = (BIN_COUNT, BIN_COUNT)
+    eye = lax.broadcasted_iota(jnp.int32, square, 0) == lax.broadcasted_iota(jnp.int32, square, 1)
+    dec_col = jnp.sum(jnp.where(eye, dec_row, 0.0), axis=1, keepdims=True)
+    det_col = jnp.sum(jnp.where(eye, det_row, 0.0), axis=1, keepdims=True)
+    lag = lane_iota((BIN_COUNT, SIDE)).astype(F32)
+
+    def power(exponent, rate, angle):
+        size = jnp.exp(-rate * exponent)
+        return size * jnp.cos(angle * exponent), -size * jnp.sin(angle * exponent)
+
+    def bin_of(q):
+        part = lax.rem(q, 64)
+        within = lax.rem(part, 16)
+        return jnp.where(within < 8, (part // 16) * 8 + within, -1)
+
+    q_row = lax.broadcasted_iota(jnp.int32, (128, BIN_COUNT), 0)
+    spread = (bin_of(q_row) == lane_iota((128, BIN_COUNT))).astype(BF16)
+    q_lane = lane_iota((BIN_COUNT, 128))
+    pick = bin_of(q_lane) == lax.broadcasted_iota(jnp.int32, (BIN_COUNT, 128), 0)
+    dec_lane = jnp.sum(jnp.where(pick, dec_col, 0.0), axis=0, keepdims=True)
+    det_lane = jnp.sum(jnp.where(pick, det_col, 0.0), axis=0, keepdims=True)
+    ahead = power(lag, dec_col, det_col)
+    is_re = lax.broadcasted_iota(jnp.int32, (128, SIDE), 0) < 64
+    (re_hi, re_lo), (im_hi, im_lo) = halves(ahead[0]), halves(ahead[1])
+    for ref, re, im in ((q_hi, re_hi, im_hi), (q_lo, re_lo, im_lo)):
+        re, im = dot(spread, re), dot(spread, im)
+        ref[:, :SIDE] = jnp.where(is_re, re, -im).astype(BF16)
+        ref[:, SIDE:] = jnp.where(is_re, im, re).astype(BF16)
+    lane = lane_iota((BIN_COUNT, SIDE))
+    inner = lax.rem(lane, 16)
+    held = jnp.where(inner < 8, (lane // 64) * 8 + inner, -1)
+    held = held == lax.broadcasted_iota(jnp.int32, (BIN_COUNT, SIDE), 0)
+    held_b = held.astype(BF16)
+    step_dec = jnp.sum(jnp.where(held, dec_col, 0.0), axis=0, keepdims=True)
+    step_det = jnp.sum(jnp.where(held, det_col, 0.0), axis=0, keepdims=True)
+    behind = power(SIDE - lag, dec_col, det_col)
+    for ref, which in ((p_hi, 0), (p_lo, 1)):
+        re = halves(behind[0])[which].astype(F32).T.astype(BF16)
+        im = halves(behind[1])[which].astype(F32).T.astype(BF16)
+        re, im = dot(re, held_b), dot(im, held_b)
+        ref[:SIDE, :SIDE] = re.astype(BF16)
+        ref[:SIDE, SIDE:] = im.astype(BF16)
+        ref[SIDE:, :SIDE] = (-im).astype(BF16)
+        ref[SIDE:, SIDE:] = re.astype(BF16)
+    y = 2.0 * dec_lane
+    series = jnp.ones_like(y)
+    for n in range(9, 1, -1):
+        series = 1.0 - series * y * (1.0 / n)
+    drive = jnp.sqrt(y * series)
+    bins_here = bin_of(lax.broadcasted_iota(jnp.int32, (128, occ.shape[0]), 0))
+    member = (bins_here == gb_ref[...]).astype(BF16)
+    occ_hi, occ_lo = halves(occ[...])
+    ct[...] = (dot(member, occ_hi) + dot(member, occ_lo)).T * drive
+
+    def wide_dft(re, im):
+        x = halves(jnp.concatenate([re, im], axis=1))
+        y = dot3(x, (wh[...], wl[...]))
+        return y[:, :SIDE], y[:, SIDE:]
+
+    def wide_inverse(re, im):
+        return conj(wide_dft(re, -im))
+
+    def row(k):
+        return rows_ref[0, k : k + 1, :], rows_ref[1, k : k + 1, :]
+
+    def stack(items):
+        return tuple(jnp.concatenate([item[c] for item in items], axis=0) for c in (0, 1))
+
+    def unstack(value):
+        return [tuple(v[ROWS * k : ROWS * (k + 1)] for v in value) for k in range(TIMES)]
+
+    def time_dft(items):
+        items = small_fft(items, -1)
+        return wide_dft(*stack([cmul(item, row(k)) for k, item in enumerate(items)]))
+
+    def time_inverse_dft(value):
+        items = unstack(wide_inverse(*value))
+        return small_fft([cmul(item, conj(row(k))) for k, item in enumerate(items)], 1)
+
+    def twist(items, back):
+        rows = [row(TIMES + k) for k in range(TIMES)]
+        return [cmul(x, conj(r) if back else r) for x, r in zip(items, rows)]
+
+    def column_dft(x, back):
+        hi, lo = halves(x)
+        w = (wh[:, :SIDE], wl[:, :SIDE])
+        y = dot3(w, (hi, lo))
+        tops, bottoms = y[:SIDE], y[SIDE:]
+        parts = []
+        for k in range(x.shape[1] // 128):
+            top, bottom = tops[:, 128 * k : 128 * k + 128], bottoms[:, 128 * k : 128 * k + 128]
+            parts.append(top + turn(bottom) if back else top - turn(bottom))
+        return parts
+
+    def diffract(groups):
+        spectrum = []
+        for x in groups:
+            a, b, c, d = x[0] + x[2], x[0] - x[2], x[1] + x[3], turn(x[1] - x[3])
+            for k, y in enumerate((a + c, b - d, a - c, b + d)):
+                spectrum.append(y * tw_c[k] + roll(y, 64) * tw_s[k] if k else y)
+        spectrum = column_dft(jnp.concatenate(spectrum, axis=1), False)
+        spectrum = [
+            y * ph_c[i % LATS] + roll(y, 64) * ph_s[i % LATS] for i, y in enumerate(spectrum)
+        ]
+        result = column_dft(jnp.concatenate(spectrum, axis=1), True)
+        done = []
+        for g in range(len(groups)):
+            x = []
+            for k in range(LATS):
+                y = result[g * LATS + k]
+                x.append(y * tw_c[k] - roll(y, 64) * tw_s[k] if k else y)
+            a, b, c, d = x[0] + x[2], x[0] - x[2], x[1] + x[3], turn(x[1] - x[3])
+            done.append([a + c, b + d, a - c, b - d])
+        return done
+
+    for d in range(1, LATS):
+        lat_recv(s1, r1, ss1, rs1, d).wait_recv()
+    for a, tile in enumerate(diffract([[r1[a] for a in range(LATS)]])[0]):
+        s2[a] = tile
+    each(to_rows, lambda copy: copy.start())
+    r2[m, l] = s2[l, pl.ds(pl.multiple_of(m * ROWS, ROWS), ROWS)]
+
+    mine = ct[pl.ds(pl.multiple_of(m * ROWS, ROWS), ROWS), :]
+    first_half = lane_iota((1, 128)) < 64
+    scaled = []
+    for k in range(TIMES):
+        far = power(float(SIDE * k), dec_lane, det_lane)
+        scaled.append(mine * jnp.where(first_half, far[0], far[1]))
+    q = (q_hi[...], q_lo[...])
+    response = dot3(halves(jnp.concatenate(scaled, axis=0)), q)
+    response = unstack((response[:, :SIDE], response[:, SIDE:]))
+    even = time_dft(response)
+    kev[0] = LONG * (1.0 - (0.5 * weight) * even[1])
+    kev[1] = (LONG * 0.5 * weight) * even[0]
+    odd = time_dft(twist(response, False))
+    kod[0] = (-0.5 * weight / LONG) * odd[1]
+    kod[1] = (0.5 * weight / LONG) * odd[0]
+
+    each(from_columns, lambda copy: copy.wait_recv())
+    field = []
+    for k in range(TIMES):
+        field.append(unpack([r2[k, a] for a in range(LATS)]))
+    turn_row = stack([
+        tuple(jnp.broadcast_to(spec[c, k : k + 1, :], (ROWS, SIDE)) for c in (0, 1))
+        for k in range(TIMES)
+    ])
+    once = cmul(time_dft(field), turn_row)
+    twisted = time_dft(twist(time_inverse_dft(once), False))
+    twisted = time_inverse_dft(cmul(twisted, (kod[0], kod[1])))
+    late = time_dft(twist(twisted, True))
+    straight = cmul(once, (kev[0], kev[1]))
+    once = cmul((straight[0] + late[0], straight[1] + late[1]), turn_row)
+    field = time_inverse_dft(once)
+    flat = stack(field)
+    ends = dot3(halves(jnp.concatenate(flat, axis=1)), (p_hi[...], p_lo[...]))
+    ends = unstack((ends[:, :SIDE], ends[:, SIDE:]))
+    step = power(float(SIDE), step_dec, step_det)
+    state = (jnp.zeros((ROWS, SIDE), F32), jnp.zeros((ROWS, SIDE), F32))
+    slot = lax.rem(lane_iota((8, SIDE)) // 16, 4)
+    for k in range(TIMES):
+        folded = []
+        for c in (0, 1):
+            total = jnp.zeros((8, SIDE), F32)
+            for g in range(4):
+                total = jnp.where(slot == g, state[c][8 * g : 8 * g + 8], total)
+            folded.append(total)
+        tiles, extra = pack(*field[k]), pack(*folded)
+        for a in range(LATS):
+            s3[k, a, :ROWS, :] = tiles[a]
+            s3[k, a, ROWS:, :] = extra[a]
+        moved = cmul(state, step)
+        state = (moved[0] + ends[k][0], moved[1] + ends[k][1])
+    each(to_columns, lambda copy: copy.start())
+    r3[l, m] = s3[m, l]
+
+    t2 = row(2 * TIMES)
+    q = (q_hi[...], q_lo[...])
+    response = dot3(halves(jnp.where(lane_iota(whole) < 64, ct[...], 0.0)), q)
+    response = (response[:, :SIDE], response[:, SIDE:])
+    even, odd = wide_dft(*response), wide_dft(*cmul(response, t2))
+    gain = 0.5 * weight / SIDE
+    kfe[0], kfe[1] = -gain * even[1], gain * even[0]
+    kfo[0], kfo[1] = -gain * odd[1], gain * odd[0]
+
+    each(from_rows, lambda copy: copy.wait_recv())
+    tiles, states = [], []
+    for a in range(LATS):
+        tiles.append(r3[a, :, :ROWS, :].reshape(SIDE, 128))
+        extra = r3[a, :, ROWS:, :].reshape(8 * TIMES, 128)
+        extra = [roll(extra, -16 * g).reshape(TIMES, 8, 128) for g in range(4)]
+        states.append(jnp.stack(extra, axis=1).reshape(SIDE, 128))
+    tiles, states = diffract([tiles, states])
+    slot = lax.rem(lane_iota((ROWS, 128)), 64) // 8
+    for a in range(LATS):
+        s4[a, :SIDE, :] = tiles[a]
+        total = jnp.zeros((ROWS, 128), F32)
+        for g in range(8):
+            total = jnp.where(slot == g, roll(states[a][ROWS * g : ROWS * (g + 1)], 8 * g), total)
+        s4[a, SIDE:, :] = total
+    last = [lat_send(s4, r4, ss4, rs4, d) for d in range(1, LATS)]
+    for copy in last:
+        copy.start()
+    r4[l] = s4[l]
+    for d in range(1, LATS):
+        lat_recv(s4, r4, ss4, rs4, d).wait_recv()
+
+    field = unpack([r4[a, :SIDE, :] for a in range(LATS)])
+    slot = lax.rem(lane_iota((ROWS, 128)), 64) // 16
+    carried = []
+    for g in range(8):
+        total = jnp.zeros((ROWS, 128), F32)
+        for a in range(LATS):
+            total = jnp.where(slot == a, roll(r4[a, SIDE:, :], 16 * a - 8 * g), total)
+        carried.append(total)
+    carried = halves(jnp.concatenate(carried, axis=0) * ct[...])
+    carried = dot3(carried, (q_hi[...], q_lo[...]))
+    even = wide_inverse(*cmul(wide_dft(*field), (kfe[0], kfe[1])))
+    odd = wide_inverse(*cmul(wide_dft(*cmul(field, t2)), (kfo[0], kfo[1])))
+    odd = cmul(odd, conj(t2))
+    out[0] = field[0] + even[0] + odd[0] - weight * carried[:, SIDE:]
+    out[1] = field[1] + even[1] + odd[1] + weight * carried[:, :SIDE]
+
+    for copy in first + last:
+        copy.wait_send()
+    each(to_rows, lambda copy: copy.wait_send())
+    each(to_columns, lambda copy: copy.wait_send())
+
+
+def fused(light_field, lateral_phase, spectral_phase, occupation, bin_decay, bin_detune, group_bin):
+    tile = (SIDE, 128)
+    vmem, sems = pltpu.VMEM, pltpu.SemaphoreType.DMA
+    exchange = [
+        vmem((LATS,) + tile, F32), vmem((LATS,) + tile, F32),
+        vmem((LATS,) + tile, F32), vmem((TIMES, LATS, ROWS, 128), F32),
+        vmem((TIMES, LATS, ROWS + 8, 128), F32), vmem((LATS, TIMES, ROWS + 8, 128), F32),
+        vmem((LATS, SIDE + ROWS, 128), F32), vmem((LATS, SIDE + ROWS, 128), F32),
+    ]
+    tables = [vmem((LATS,) + tile, F32)] * 4 + [vmem(tile, F32)]
+    tables += [vmem((128, 2 * SIDE), BF16)] * 2 + [vmem((2 * SIDE, 2 * SIDE), BF16)] * 2
+    tables += [vmem((2, SIDE, SIDE), F32)] * 4 + [vmem((2, TIMES, SIDE), F32)]
+    semaphores = [sems((LATS,))] * 2 + [sems((TOTAL,))] * 4 + [sems((LATS,))] * 2
+    return pl.pallas_call(
+        kernel,
+        out_shape=jax.ShapeDtypeStruct(light_field.shape, F32),
+        in_specs=[pl.BlockSpec(memory_space=pltpu.VMEM)] * 11,
+        out_specs=pl.BlockSpec(memory_space=pltpu.VMEM),
+        scratch_shapes=exchange + tables + semaphores,
+        compiler_params=pltpu.CompilerParams(
+            collective_id=0, has_side_effects=True, vmem_limit_bytes=50 * 1024 * 1024
+        ),
+    )(
+        light_field,
+        lateral_phase.reshape(SIDE, LATS),
+        spectral_phase.reshape(SIDE, TIMES).T,
+        occupation,
+        bin_decay[None],
+        bin_detune[None],
+        group_bin[None],
+        *[jnp.asarray(c) for c in constants()],
+    )
+
+
 def solution(mesh):
+    def local(light_field, *rest):
+        fits = (lax.axis_size("lat"), lax.axis_size("tm")) == (LATS, TIMES)
+        fits = fits and light_field.shape == (2, SIDE, SIDE)
+        fits = fits and rest[2].shape == (128, SIDE) and rest[3].shape == (BIN_COUNT,)
+        return (fused if fits else on_device)(light_field, *rest)
+
     return jax.shard_map(
-        on_device,
+        local,
         mesh=mesh,
         in_specs=(P(None, "lat", "tm"), P(), P(), P(None, "lat"), P(), P(), P()),
         out_specs=P(None, "lat", "tm"),

time: 978 us -> 73.2 us (0.07)
  matrix products: 588 us -> 0 us
  local copies, waits for them, and re-layouts: 205 us -> 6.24 us
  Pallas kernels: 0 us -> 66.6 us
  blocking collectives: 61 us -> 0 us
  waiting for transfers between devices: 42.9 us -> 0 us
  other arithmetic: 35 us -> 0 us
  starting transfers between devices: 21.1 us -> 0 us
  between operations: 15.2 us -> 0.05 us
    dot_general x76 -> x0, matrix products: 588 us -> none  [the longest x18 147 us: complex_einsum(): jnp.einsum(form, left[1], right[1], precision=exact)]
    gather x4 -> x0, local copies, waits for them, and re-layouts: 160 us -> none  [the longest x2 80.2 us: on_device(): jnp.take(jnp.dot(coupling.T, lag_powers[0][:STRETCH].T, precision=exact),...]
    pallas_call x0 -> x1, Pallas kernels: none -> 66.6 us  [fused(): pl.pallas_call(kernel, out_shape=jax.ShapeDtypeStruct(light_field.shape,...]
    all_to_all x5 -> x0, waiting for transfers between devices: 42.7 us -> none  [the longest x2 15.2 us: on_device(): lax.all_to_all(joined, 'tm', split_axis=3, concat_axis=1, tiled=True)]
    all_to_all x3 -> x0, blocking collectives: 40.4 us -> none  [the longest x1 18.2 us: on_device(): lax.all_to_all(stacked, 'tm', split_axis=1, concat_axis=3, tiled=True)[:, 0]]
    all_to_all x5 -> x0, starting transfers between devices: 20.9 us -> none  [the longest x2 6.99 us: on_device(): lax.all_to_all(joined, 'tm', split_axis=3, concat_axis=1, tiled=True)]
    all_gather x2 -> x0, blocking collectives: 20.6 us -> none  [carried_in(): pieces = jax.tree.map(lambda part: lax.all_gather(part, axis), value)]
    unnamed x76 -> x23, local copies, waits for them, and re-layouts: 23.9 us -> 5.96 us
  transfers between devices with their start and end apart: 9 -> 0, of which waited for: 4 -> 0; matrix products, arithmetic and copies ran while one was open for 41% -> 0% of each run, Pallas kernels for 0% -> 0%
where the time goes in v1:
time: 73.2 us; the launch traced here: 72.9 us
  Pallas kernels  66.6 us (91%)
  local copies, waits for them, and re-layouts  6.24 us (9%)
    pallas_call x1, Pallas kernels, fused(): pl.pallas_call(kernel, out_shape=jax.ShapeDtypeStruct(light_field.shape,...  66.6 us
    unnamed x23, local copies, waits for them, and re-layouts  5.96 us

profile of v1, /device:TPU:0, one launch (start us, length us, event | category | flops | bytes accessed | tf_op | source)
XLA Modules:
  0.0 72.9 jit_solution(8643186527913742179)
XLA Ops:
  0.0 0.0 copy-start.10
  0.0 0.7 copy-done.10
  0.7 0.0 copy-start.9
  0.7 0.0 copy-start.5
  0.7 0.1 reshape.6.latp
  0.8 0.6 copy-done.9
  1.4 0.0 copy-start.3
  1.4 0.0 copy-start.4
  1.4 0.1 reshape.7
  1.5 0.1 copy.12
  1.6 0.0 copy-start.6
  1.6 0.0 copy-start.7
  1.6 0.0 copy-start.8
  1.6 0.0 copy-done.5
  1.6 0.7 copy-done.3
  2.3 0.1 copy-done.4
  2.4 0.0 copy-done.6
  2.4 0.0 copy-done.7
  2.4 0.0 copy-done.8
  2.4 0.0 copy-start
  2.4 1.0 %copy-done = f32[2,256,256]{2,1,0:T(8,128)S(1)} copy-done((f32[2,256,256]{2,1,0:T(8,128)S(1)}, f32[2,256,256]{2,1,0:T(8,128)}, u32[]{:S(2)}) %copy-start) | copy-done | bytes 524312
  3.4 0.0 copy-start.1
  3.4 1.0 %copy-done.1 = bf16[512,512]{1,0:T(8,128)(2,1)S(1)} copy-done((bf16[512,512]{1,0:T(8,128)(2,1)S(1)}, bf16[512,512]{1,0:T(8,128)(2,1)}, u32[]{:S(2)}) %copy-start.1) | copy-done | bytes 524312
  4.5 0.0 copy-start.2
  4.5 1.0 %copy-done.2 = bf16[512,512]{1,0:T(8,128)(2,1)S(1)} copy-done((bf16[512,512]{1,0:T(8,128)(2,1)S(1)}, bf16[512,512]{1,0:T(8,128)(2,1)}, u32[]{:S(2)}) %copy-start.2) | copy-done | bytes 524312
  5.5 66.6 %shard_map.109 = f32[2,256,256]{2,1,0:T(8,128)S(1)} custom-call(f32[2,256,256]{2,1,0:T(8,128)S(1)} %copy-done, f32[256,4]{1,0:T(8,128)S(1)} %reshape.6.latp, f32[8,256]{1,0:T(8,128)S(1)} %bitcast.4, f32[128,256]{1,0:T(8,128)S(1)} %copy-done.3, f32[1,32]{1,0:T(1,128)S(1)} %bitcast.5, f32[1,32]{1,0:T(1,128)S(1)} %bitcast.6, s32[1,128]{1,0:T(1,128)S(1)} %bitcast.7, ...), custom_call_target="tpu_custom_call" | custom-call | tf_op jit(solution)/shard_map/pallas_call | solution.py:638
  72.1 0.8 %copy.14 = f32[2,256,256]{2,1,0:T(8,128)} copy(f32[2,256,256]{2,1,0:T(8,128)S(1)} %shard_map.109) | data formatting | bytes 1048576
Async XLA Ops:
  0.0 0.7 copy-start.10
  0.7 0.7 copy-start.9
  0.7 0.9 %copy-start.5 = (f32[2,24,256]{2,1,0:T(8,128)S(1)}, f32[2,24,256]{2,1,0:T(8,128)}, u32[]{:S(2)}) copy-start(f32[2,24,256]{2,1,0:T(8,128)} %constant.10.clone.rows_ref) | copy-start | bytes 147460
  1.4 0.9 %copy-start.3 = (f32[128,256]{1,0:T(8,128)S(1)}, f32[128,256]{1,0:T(8,128)}, u32[]{:S(2)}) copy-start(f32[128,256]{1,0:T(8,128)} %occ.1) | copy-start | bytes 393220
  1.4 1.0 %copy-start.4 = (f32[256,8]{1,0:T(8,128)S(1)}, f32[256,8]{1,0:T(8,128)}, u32[]{:S(2)}) copy-start(f32[256,8]{1,0:T(8,128)} %constant.11.clone.cols_ref) | copy-start | bytes 24580
  1.6 0.8 %copy-start.6 = (f32[32]{0:T(128)S(1)}, f32[32]{0:T(128)}, u32[]{:S(2)}) copy-start(f32[32]{0:T(128)} %param.15) | copy-start | bytes 388
  1.6 0.8 %copy-start.7 = (f32[32]{0:T(128)S(1)}, f32[32]{0:T(128)}, u32[]{:S(2)}) copy-start(f32[32]{0:T(128)} %param.16) | copy-start | bytes 388
  1.6 0.8 %copy-start.8 = (s32[128]{0:T(128)S(1)}, s32[128]{0:T(128)}, u32[]{:S(2)}) copy-start(s32[128]{0:T(128)} %param.17) | copy-start | bytes 1540
  2.4 1.0 %copy-start = (f32[2,256,256]{2,1,0:T(8,128)S(1)}, f32[2,256,256]{2,1,0:T(8,128)}, u32[]{:S(2)}) copy-start(f32[2,256,256]{2,1,0:T(8,128)} %lf.1) | copy-start | bytes 1572868
  3.4 1.0 %copy-start.1 = (bf16[512,512]{1,0:T(8,128)(2,1)S(1)}, bf16[512,512]{1,0:T(8,128)(2,1)}, u32[]{:S(2)}) copy-start(bf16[512,512]{1,0:T(8,128)(2,1)} %constant.9.clone.wl) | copy-start | bytes 1572868
  4.5 1.0 %copy-start.2 = (bf16[512,512]{1,0:T(8,128)(2,1)S(1)}, bf16[512,512]{1,0:T(8,128)(2,1)}, u32[]{:S(2)}) copy-start(bf16[512,512]{1,0:T(8,128)(2,1)} %constant.8.clone.wh) | copy-start | bytes 1572868

commit v2 on v1

--- a/solution.py
+++ b/solution.py
@@ -213,6 +213,7 @@
 WIDE = LATS * SIDE
 LONG = TIMES * SIDE
 ROWS = SIDE // TIMES
+PART = ROWS // 2
 F32, BF16 = jnp.float32, jnp.bfloat16
 MESH = pl.DeviceIdType.MESH
 
@@ -312,28 +313,49 @@
 
 
 def kernel(
-    lf, latp, specp, occ, dec_ref, det_ref, gb_ref, wh, wl, rows_ref, cols_ref,
+    lf_hbm, latp, specp, occ_hbm, dec_ref, det_ref, gb_ref, wh_hbm, wl_hbm, rows_hbm, cols_hbm,
     out,
-    s1, r1, s2, r2, s3, r3, s4, r4,
+    s1, r1, s2, r2, s3a, r3a, s3b, r3b, s4, r4,
     tw_c, tw_s, ph_c, ph_s, ct, q_hi, q_lo, p_hi, p_lo, kev, kod, kfe, kfo, spec,
-    ss1, rs1, ss2, rs2, ss3, rs3, ss4, rs4,
+    lf, occ, wh, wl, rows_ref, cols_ref,
+    ss1, rs1, ss2, rs2, ss3, rs3, ss4, rs4, load_sem,
 ):
+    loads = []
+    for i, (src, dst) in enumerate((
+        (lf_hbm, lf), (cols_hbm, cols_ref), (wh_hbm, wh), (wl_hbm, wl), (occ_hbm, occ),
+        (rows_hbm, rows_ref),
+    )):
+        loads.append(pltpu.make_async_copy(src, dst, load_sem.at[i]))
+        loads[-1].start()
     l, m = lax.axis_index("lat"), lax.axis_index("tm")
     me = l * TIMES + m
     weight = GAIN_SCALE / math.sqrt(occ.shape[0])
 
+    half = TIMES // 2
+
     def other(d):
-        t = lax.rem(me + d, TOTAL)
-        return t, t // TIMES, lax.rem(t, TIMES)
+        side = lax.rem(m // half + 1 + d // (TOTAL // 2), 2)
+        tm = side * half + lax.rem(m + d, half)
+        tl = lax.rem(l + lax.rem(d // half, LATS), LATS)
+        return tl * TIMES + tm, tl, tm
+
+    def each(act):
+        act(0)
+
+        def body(d, carry):
+            act(d)
+            act(d + TOTAL // 2)
+            return carry
+
+        lax.fori_loop(1, TOTAL // 2, body, 0)
 
     barrier = pltpu.get_barrier_semaphore()
 
-    def greet(d, carry):
+    def greet(d):
         t, tl, tm = other(d)
         pl.semaphore_signal(barrier, inc=1, device_id=(tl, tm), device_id_type=MESH)
-        return carry
-
-    lax.fori_loop(1, TOTAL, greet, 0)
+
+    each(greet)
 
     def remote(src, dst, send, recv, tl, tm):
         return pltpu.make_async_remote_copy(
@@ -349,30 +371,27 @@
         t = lax.rem(l + d, LATS)
         return remote(s.at[t], r.at[t], ss.at[t], rs.at[t], t, m)
 
-    def to_rows(d):
+    def to_rows(h, d):
         t, tl, tm = other(d)
-        src = s2.at[tl, pl.ds(pl.multiple_of(tm * ROWS, ROWS), ROWS)]
-        return remote(src, r2.at[m, l], ss2.at[t], rs2.at[me], tl, tm)
-
-    def from_columns(d):
+        src = s2.at[tl, pl.ds(pl.multiple_of(tm * ROWS + h * PART, PART), PART)]
+        return remote(src, r2.at[h, m, l], ss2.at[h, t], rs2.at[h, me], tl, tm)
+
+    def from_columns(h, d):
         t, tl, tm = other(d)
-        return remote(r2.at[tm, tl], r2.at[tm, tl], ss2.at[t], rs2.at[t], tl, tm)
-
-    def to_columns(d):
+        return remote(r2.at[h, tm, tl], r2.at[h, tm, tl], ss2.at[h, t], rs2.at[h, t], tl, tm)
+
+    s3, r3 = (s3a, s3b), (r3a, r3b)
+
+    def to_columns(h, d):
         t, tl, tm = other(d)
-        return remote(s3.at[tm, tl], r3.at[l, m], ss3.at[t], rs3.at[me], tl, tm)
-
-    def from_rows(d):
+        return remote(s3[h].at[tm, tl], r3[h].at[l, m], ss3.at[h, t], rs3.at[h, me], tl, tm)
+
+    def from_rows(h, d):
         t, tl, tm = other(d)
-        return remote(r3.at[tl, tm], r3.at[tl, tm], ss3.at[t], rs3.at[t], tl, tm)
-
-    def each(make, act):
-        def body(d, carry):
-            act(make(d))
-            return carry
-
-        lax.fori_loop(1, TOTAL, body, 0)
-
+        here = r3[h].at[tl, tm]
+        return remote(here, here, ss3.at[h, t], rs3.at[h, t], tl, tm)
+
+    loads[0].wait()
     for t, tile in enumerate(pack(lf[0], lf[1])):
         s1[t] = tile
     pl.semaphore_wait(barrier, TOTAL - 1)
@@ -381,7 +400,9 @@
         copy.start()
     r1[l] = s1[l]
 
+    loads[1].wait()
     whole = (SIDE, 128)
+    group = lax.rem(lane_iota(whole), 64) // 16
     sign = jnp.where(lane_iota(whole) < 64, -1.0, 1.0)
     phase = latp[...]
     turn_c, turn_s = jnp.cos(phase) * (1.0 / WIDE), jnp.sin(phase) * (1.0 / WIDE)
@@ -390,6 +411,99 @@
         tw_s[k] = jnp.broadcast_to(cols_ref[:, LATS + k : LATS + k + 1], whole) * sign
         ph_c[k] = jnp.broadcast_to(turn_c[:, k : k + 1], whole)
         ph_s[k] = jnp.broadcast_to(turn_s[:, k : k + 1], whole) * sign
+
+    def wide_dft(re, im):
+        x = halves(jnp.concatenate([re, im], axis=1))
+        y = dot3(x, (wh[...], wl[...]))
+        return y[:, :SIDE], y[:, SIDE:]
+
+    def wide_inverse(re, im):
+        return conj(wide_dft(re, -im))
+
+    def row(k):
+        return rows_ref[0, k : k + 1, :], rows_ref[1, k : k + 1, :]
+
+    def stack(items):
+        return tuple(jnp.concatenate([item[c] for item in items], axis=0) for c in (0, 1))
+
+    def unstack(value):
+        return [tuple(v[PART * k : PART * (k + 1)] for v in value) for k in range(TIMES)]
+
+    def time_dft(items):
+        items = small_fft(items, -1)
+        return wide_dft(*stack([cmul(item, row(k)) for k, item in enumerate(items)]))
+
+    def time_inverse_dft(value):
+        items = unstack(wide_inverse(*value))
+        return small_fft([cmul(item, conj(row(k))) for k, item in enumerate(items)], 1)
+
+    def twist(items, back):
+        rows = [row(TIMES + k) for k in range(TIMES)]
+        return [cmul(x, conj(r) if back else r) for x, r in zip(items, rows)]
+
+    def column_dft(x, low, high):
+        w = [
+            jnp.concatenate([ref[low:high, :SIDE], ref[SIDE + low : SIDE + high, :SIDE]], axis=0)
+            for ref in (wh, wl)
+        ]
+        y = dot3(w, halves(x))
+        count = high - low
+        return [
+            (y[:count, k : k + 128], y[count:, k : k + 128]) for k in range(0, x.shape[1], 128)
+        ]
+
+    def lateral_spectrum(x, states):
+        spectrum = []
+        for x in (x, states) if states else (x,):
+            a, b, c, d = x[0] + x[2], x[0] - x[2], x[1] + x[3], turn(x[1] - x[3])
+            for k, y in enumerate((a + c, b - d, a - c, b + d)):
+                spectrum.append(y * tw_c[k] + roll(y, 64) * tw_s[k] if k else y)
+        turns = [(ph_c[k], ph_s[k]) for k in range(LATS)]
+        if states:
+            tile, across, along = spectrum[LATS], turns[0][0], turns[0][1]
+            for k in range(1, LATS):
+                tile = jnp.where(group == k, roll(spectrum[LATS + k], 16 * k), tile)
+                across = jnp.where(group == k, turns[k][0], across)
+                along = jnp.where(group == k, turns[k][1], along)
+            spectrum[LATS:] = [tile]
+            turns.append((across, along))
+        spectrum = column_dft(jnp.concatenate(spectrum, axis=1), 0, SIDE)
+        done = []
+        for (top, bottom), (across, along) in zip(spectrum, turns):
+            y = top - turn(bottom)
+            done.append(y * across + roll(y, 64) * along)
+        return jnp.concatenate(done, axis=1)
+
+    def lateral_inverse(spectrum, low, high):
+        result = [top + turn(bottom) for top, bottom in column_dft(spectrum, low, high)]
+        groups = [result[:LATS]]
+        if len(result) > LATS:
+            groups.append([roll(result[LATS], -16 * k) for k in range(LATS)])
+        done = []
+        for result in groups:
+            x = []
+            for k, y in enumerate(result):
+                if k:
+                    y = y * tw_c[k, low:high, :] - roll(y, 64) * tw_s[k, low:high, :]
+                x.append(y)
+            a, b, c, d = x[0] + x[2], x[0] - x[2], x[1] + x[3], turn(x[1] - x[3])
+            done.append([a + c, b + d, a - c, b - d])
+        return done
+
+    loads[2].wait()
+    loads[3].wait()
+    for d in range(1, LATS):
+        lat_recv(s1, r1, ss1, rs1, d).wait_recv()
+    spectrum = lateral_spectrum([r1[a] for a in range(LATS)], None)
+    for a, tile in enumerate(lateral_inverse(spectrum, 0, SIDE)[0]):
+        s2[a] = tile
+    for h in range(2):
+        each(lambda d, h=h: to_rows(h, d).start())
+    for h in range(2):
+        r2[h, m, l] = s2[l, pl.ds(pl.multiple_of(m * ROWS + h * PART, PART), PART)]
+
+    loads[4].wait()
+    loads[5].wait()
     spec[0] = jnp.cos(specp[...]) * (1.0 / LONG)
     spec[1] = jnp.sin(specp[...]) * (1.0 / LONG)
 
@@ -448,128 +562,64 @@
     occ_hi, occ_lo = halves(occ[...])
     ct[...] = (dot(member, occ_hi) + dot(member, occ_lo)).T * drive
 
-    def wide_dft(re, im):
-        x = halves(jnp.concatenate([re, im], axis=1))
-        y = dot3(x, (wh[...], wl[...]))
-        return y[:, :SIDE], y[:, SIDE:]
-
-    def wide_inverse(re, im):
-        return conj(wide_dft(re, -im))
-
-    def row(k):
-        return rows_ref[0, k : k + 1, :], rows_ref[1, k : k + 1, :]
-
-    def stack(items):
-        return tuple(jnp.concatenate([item[c] for item in items], axis=0) for c in (0, 1))
-
-    def unstack(value):
-        return [tuple(v[ROWS * k : ROWS * (k + 1)] for v in value) for k in range(TIMES)]
-
-    def time_dft(items):
-        items = small_fft(items, -1)
-        return wide_dft(*stack([cmul(item, row(k)) for k, item in enumerate(items)]))
-
-    def time_inverse_dft(value):
-        items = unstack(wide_inverse(*value))
-        return small_fft([cmul(item, conj(row(k))) for k, item in enumerate(items)], 1)
-
-    def twist(items, back):
-        rows = [row(TIMES + k) for k in range(TIMES)]
-        return [cmul(x, conj(r) if back else r) for x, r in zip(items, rows)]
-
-    def column_dft(x, back):
-        hi, lo = halves(x)
-        w = (wh[:, :SIDE], wl[:, :SIDE])
-        y = dot3(w, (hi, lo))
-        tops, bottoms = y[:SIDE], y[SIDE:]
-        parts = []
-        for k in range(x.shape[1] // 128):
-            top, bottom = tops[:, 128 * k : 128 * k + 128], bottoms[:, 128 * k : 128 * k + 128]
-            parts.append(top + turn(bottom) if back else top - turn(bottom))
-        return parts
-
-    def diffract(groups):
-        spectrum = []
-        for x in groups:
-            a, b, c, d = x[0] + x[2], x[0] - x[2], x[1] + x[3], turn(x[1] - x[3])
-            for k, y in enumerate((a + c, b - d, a - c, b + d)):
-                spectrum.append(y * tw_c[k] + roll(y, 64) * tw_s[k] if k else y)
-        spectrum = column_dft(jnp.concatenate(spectrum, axis=1), False)
-        spectrum = [
-            y * ph_c[i % LATS] + roll(y, 64) * ph_s[i % LATS] for i, y in enumerate(spectrum)
-        ]
-        result = column_dft(jnp.concatenate(spectrum, axis=1), True)
-        done = []
-        for g in range(len(groups)):
-            x = []
-            for k in range(LATS):
-                y = result[g * LATS + k]
-                x.append(y * tw_c[k] - roll(y, 64) * tw_s[k] if k else y)
-            a, b, c, d = x[0] + x[2], x[0] - x[2], x[1] + x[3], turn(x[1] - x[3])
-            done.append([a + c, b + d, a - c, b - d])
-        return done
-
-    for d in range(1, LATS):
-        lat_recv(s1, r1, ss1, rs1, d).wait_recv()
-    for a, tile in enumerate(diffract([[r1[a] for a in range(LATS)]])[0]):
-        s2[a] = tile
-    each(to_rows, lambda copy: copy.start())
-    r2[m, l] = s2[l, pl.ds(pl.multiple_of(m * ROWS, ROWS), ROWS)]
-
-    mine = ct[pl.ds(pl.multiple_of(m * ROWS, ROWS), ROWS), :]
     first_half = lane_iota((1, 128)) < 64
-    scaled = []
+    far = []
     for k in range(TIMES):
-        far = power(float(SIDE * k), dec_lane, det_lane)
-        scaled.append(mine * jnp.where(first_half, far[0], far[1]))
-    q = (q_hi[...], q_lo[...])
-    response = dot3(halves(jnp.concatenate(scaled, axis=0)), q)
-    response = unstack((response[:, :SIDE], response[:, SIDE:]))
-    even = time_dft(response)
-    kev[0] = LONG * (1.0 - (0.5 * weight) * even[1])
-    kev[1] = (LONG * 0.5 * weight) * even[0]
-    odd = time_dft(twist(response, False))
-    kod[0] = (-0.5 * weight / LONG) * odd[1]
-    kod[1] = (0.5 * weight / LONG) * odd[0]
-
-    each(from_columns, lambda copy: copy.wait_recv())
-    field = []
+        far.append(jnp.where(first_half, *power(float(SIDE * k), dec_lane, det_lane)))
+    for h in range(2):
+        mine = ct[pl.ds(pl.multiple_of(m * ROWS + h * PART, PART), PART), :]
+        q = (q_hi[...], q_lo[...])
+        response = jnp.concatenate([mine * f for f in far], axis=0)
+        response = dot3(halves(response), q)
+        response = unstack((response[:, :SIDE], response[:, SIDE:]))
+        even = time_dft(response)
+        kev[h, 0] = LONG * (1.0 - (0.5 * weight) * even[1])
+        kev[h, 1] = (LONG * 0.5 * weight) * even[0]
+        odd = time_dft(twist(response, False))
+        kod[h, 0] = (-0.5 * weight / LONG) * odd[1]
+        kod[h, 1] = (0.5 * weight / LONG) * odd[0]
+
+    step = power(float(SIDE), step_dec, step_det)
+    slot = lax.rem(lane_iota((8, SIDE)) // 16, 4)
+    folded = [[jnp.zeros((8, SIDE), F32) for c in (0, 1)] for k in range(TIMES)]
+    for h in range(2):
+        each(lambda d, h=h: from_columns(h, d).wait_recv())
+        field = [unpack([r2[h, k, a] for a in range(LATS)]) for k in range(TIMES)]
+        turn_row = stack([
+            tuple(jnp.broadcast_to(spec[c, k : k + 1, :], (PART, SIDE)) for c in (0, 1))
+            for k in range(TIMES)
+        ])
+        once = cmul(time_dft(field), turn_row)
+        twisted = time_dft(twist(time_inverse_dft(once), False))
+        twisted = time_inverse_dft(cmul(twisted, (kod[h, 0], kod[h, 1])))
+        late = time_dft(twist(twisted, True))
+        straight = cmul(once, (kev[h, 0], kev[h, 1]))
+        once = cmul((straight[0] + late[0], straight[1] + late[1]), turn_row)
+        field = time_inverse_dft(once)
+        for k in range(TIMES):
+            for a, tile in enumerate(pack(*field[k])):
+                s3[h][k, a, :PART, :] = tile
+        if h == 0:
+            each(lambda d: to_columns(0, d).start())
+        flat = stack(field)
+        ends = dot3(halves(jnp.concatenate(flat, axis=1)), (p_hi[...], p_lo[...]))
+        ends = unstack((ends[:, :SIDE], ends[:, SIDE:]))
+        state = (jnp.zeros((PART, SIDE), F32), jnp.zeros((PART, SIDE), F32))
+        for k in range(TIMES):
+            for c in (0, 1):
+                for g in range(2):
+                    piece = state[c][8 * g : 8 * g + 8]
+                    folded[k][c] = jnp.where(slot == 2 * h + g, piece, folded[k][c])
+            moved = cmul(state, step)
+            state = (moved[0] + ends[k][0], moved[1] + ends[k][1])
     for k in range(TIMES):
-        field.append(unpack([r2[k, a] for a in range(LATS)]))
-    turn_row = stack([
-        tuple(jnp.broadcast_to(spec[c, k : k + 1, :], (ROWS, SIDE)) for c in (0, 1))
-        for k in range(TIMES)
-    ])
-    once = cmul(time_dft(field), turn_row)
-    twisted = time_dft(twist(time_inverse_dft(once), False))
-    twisted = time_inverse_dft(cmul(twisted, (kod[0], kod[1])))
-    late = time_dft(twist(twisted, True))
-    straight = cmul(once, (kev[0], kev[1]))
-    once = cmul((straight[0] + late[0], straight[1] + late[1]), turn_row)
-    field = time_inverse_dft(once)
-    flat = stack(field)
-    ends = dot3(halves(jnp.concatenate(flat, axis=1)), (p_hi[...], p_lo[...]))
-    ends = unstack((ends[:, :SIDE], ends[:, SIDE:]))
-    step = power(float(SIDE), step_dec, step_det)
-    state = (jnp.zeros((ROWS, SIDE), F32), jnp.zeros((ROWS, SIDE), F32))
-    slot = lax.rem(lane_iota((8, SIDE)) // 16, 4)
-    for k in range(TIMES):
-        folded = []
-        for c in (0, 1):
-            total = jnp.zeros((8, SIDE), F32)
-            for g in range(4):
-                total = jnp.where(slot == g, state[c][8 * g : 8 * g + 8], total)
-            folded.append(total)
-        tiles, extra = pack(*field[k]), pack(*folded)
-        for a in range(LATS):
-            s3[k, a, :ROWS, :] = tiles[a]
-            s3[k, a, ROWS:, :] = extra[a]
-        moved = cmul(state, step)
-        state = (moved[0] + ends[k][0], moved[1] + ends[k][1])
-    each(to_columns, lambda copy: copy.start())
-    r3[l, m] = s3[m, l]
-
-    t2 = row(2 * TIMES)
+        for a, tile in enumerate(pack(*folded[k])):
+            s3b[k, a, PART:, :] = tile
+    each(lambda d: to_columns(1, d).start())
+    for h in range(2):
+        r3[h][l, m] = s3[h][m, l]
+
+    t2 = rows_ref[0, 2 * TIMES : 2 * TIMES + 1, :], rows_ref[1, 2 * TIMES : 2 * TIMES + 1, :]
     q = (q_hi[...], q_lo[...])
     response = dot3(halves(jnp.where(lane_iota(whole) < 64, ct[...], 0.0)), q)
     response = (response[:, :SIDE], response[:, SIDE:])
@@ -578,48 +628,61 @@
     kfe[0], kfe[1] = -gain * even[1], gain * even[0]
     kfo[0], kfo[1] = -gain * odd[1], gain * odd[0]
 
-    each(from_rows, lambda copy: copy.wait_recv())
+    for h in range(2):
+        each(lambda d, h=h: from_rows(h, d).wait_recv())
     tiles, states = [], []
     for a in range(LATS):
-        tiles.append(r3[a, :, :ROWS, :].reshape(SIDE, 128))
-        extra = r3[a, :, ROWS:, :].reshape(8 * TIMES, 128)
+        both = jnp.stack([r3a[a], r3b[a, :, :PART, :]], axis=1)
+        tiles.append(both.reshape(SIDE, 128))
+        extra = r3b[a, :, PART:, :].reshape(8 * TIMES, 128)
         extra = [roll(extra, -16 * g).reshape(TIMES, 8, 128) for g in range(4)]
         states.append(jnp.stack(extra, axis=1).reshape(SIDE, 128))
-    tiles, states = diffract([tiles, states])
-    slot = lax.rem(lane_iota((ROWS, 128)), 64) // 8
-    for a in range(LATS):
-        s4[a, :SIDE, :] = tiles[a]
-        total = jnp.zeros((ROWS, 128), F32)
+    spectrum = lateral_spectrum(tiles, states)
+    span = SIDE // 2
+    fold = span // 8
+    slot = lax.rem(lane_iota((fold, 128)), 64) // 8
+    last = []
+    for h in range(2):
+        tiles, states = lateral_inverse(spectrum, span * h, span * (h + 1))
+        for a in range(LATS):
+            s4[h, a, :span, :] = tiles[a]
+            total = jnp.zeros((fold, 128), F32)
+            for g in range(8):
+                piece = roll(states[a][fold * g : fold * (g + 1)], 8 * g)
+                total = jnp.where(slot == g, piece, total)
+            s4[h, a, span:, :] = total
+        for d in range(1, LATS):
+            last.append(lat_send(s4.at[h], r4.at[h], ss4.at[h], rs4.at[h], d))
+            last[-1].start()
+        r4[h, l] = s4[h, l]
+
+    slot = lax.rem(lane_iota((fold, 128)), 64) // 16
+    for h in range(2):
+        for d in range(1, LATS):
+            lat_recv(s4.at[h], r4.at[h], ss4.at[h], rs4.at[h], d).wait_recv()
+        here = pl.ds(span * h, span)
+        field = unpack([r4[h, a, :span, :] for a in range(LATS)])
+        carried = []
         for g in range(8):
-            total = jnp.where(slot == g, roll(states[a][ROWS * g : ROWS * (g + 1)], 8 * g), total)
-        s4[a, SIDE:, :] = total
-    last = [lat_send(s4, r4, ss4, rs4, d) for d in range(1, LATS)]
-    for copy in last:
-        copy.start()
-    r4[l] = s4[l]
-    for d in range(1, LATS):
-        lat_recv(s4, r4, ss4, rs4, d).wait_recv()
-
-    field = unpack([r4[a, :SIDE, :] for a in range(LATS)])
-    slot = lax.rem(lane_iota((ROWS, 128)), 64) // 16
-    carried = []
-    for g in range(8):
-        total = jnp.zeros((ROWS, 128), F32)
-        for a in range(LATS):
-            total = jnp.where(slot == a, roll(r4[a, SIDE:, :], 16 * a - 8 * g), total)
-        carried.append(total)
-    carried = halves(jnp.concatenate(carried, axis=0) * ct[...])
-    carried = dot3(carried, (q_hi[...], q_lo[...]))
-    even = wide_inverse(*cmul(wide_dft(*field), (kfe[0], kfe[1])))
-    odd = wide_inverse(*cmul(wide_dft(*cmul(field, t2)), (kfo[0], kfo[1])))
-    odd = cmul(odd, conj(t2))
-    out[0] = field[0] + even[0] + odd[0] - weight * carried[:, SIDE:]
-    out[1] = field[1] + even[1] + odd[1] + weight * carried[:, :SIDE]
+            total = jnp.zeros((fold, 128), F32)
+            for a in range(LATS):
+                piece = roll(r4[h, a, span:, :], 16 * a - 8 * g)
+                total = jnp.where(slot == a, piece, total)
+            carried.append(total)
+        carried = halves(jnp.concatenate(carried, axis=0) * ct[here, :])
+        carried = dot3(carried, (q_hi[...], q_lo[...]))
+        even = wide_inverse(*cmul(wide_dft(*field), (kfe[0, here, :], kfe[1, here, :])))
+        odd = wide_dft(*cmul(field, t2))
+        odd = wide_inverse(*cmul(odd, (kfo[0, here, :], kfo[1, here, :])))
+        odd = cmul(odd, conj(t2))
+        out[0, here, :] = field[0] + even[0] + odd[0] - weight * carried[:, SIDE:]
+        out[1, here, :] = field[1] + even[1] + odd[1] + weight * carried[:, :SIDE]
 
     for copy in first + last:
         copy.wait_send()
-    each(to_rows, lambda copy: copy.wait_send())
-    each(to_columns, lambda copy: copy.wait_send())
+    for h in range(2):
+        each(lambda d, h=h: to_rows(h, d).wait_send())
+        each(lambda d, h=h: to_columns(h, d).wait_send())
 
 
 def fused(light_field, lateral_phase, spectral_phase, occupation, bin_decay, bin_detune, group_bin):
@@ -627,22 +690,29 @@
     vmem, sems = pltpu.VMEM, pltpu.SemaphoreType.DMA
     exchange = [
         vmem((LATS,) + tile, F32), vmem((LATS,) + tile, F32),
-        vmem((LATS,) + tile, F32), vmem((TIMES, LATS, ROWS, 128), F32),
-        vmem((TIMES, LATS, ROWS + 8, 128), F32), vmem((LATS, TIMES, ROWS + 8, 128), F32),
-        vmem((LATS, SIDE + ROWS, 128), F32), vmem((LATS, SIDE + ROWS, 128), F32),
+        vmem((LATS,) + tile, F32), vmem((2, TIMES, LATS, PART, 128), F32),
+        vmem((TIMES, LATS, PART, 128), F32), vmem((LATS, TIMES, PART, 128), F32),
+        vmem((TIMES, LATS, PART + 8, 128), F32), vmem((LATS, TIMES, PART + 8, 128), F32),
+        vmem((2, LATS, 9 * SIDE // 16, 128), F32), vmem((2, LATS, 9 * SIDE // 16, 128), F32),
     ]
     tables = [vmem((LATS,) + tile, F32)] * 4 + [vmem(tile, F32)]
     tables += [vmem((128, 2 * SIDE), BF16)] * 2 + [vmem((2 * SIDE, 2 * SIDE), BF16)] * 2
-    tables += [vmem((2, SIDE, SIDE), F32)] * 4 + [vmem((2, TIMES, SIDE), F32)]
-    semaphores = [sems((LATS,))] * 2 + [sems((TOTAL,))] * 4 + [sems((LATS,))] * 2
+    tables += [vmem((2, 2, SIDE // 2, SIDE), F32)] * 2 + [vmem((2, SIDE, SIDE), F32)] * 2
+    tables += [vmem((2, TIMES, SIDE), F32)]
+    fixed = constants()
+    tables += [vmem(light_field.shape, F32), vmem(occupation.shape, F32)]
+    tables += [vmem(c.shape, c.dtype) for c in fixed]
+    semaphores = [sems((LATS,))] * 2 + [sems((2, TOTAL))] * 4 + [sems((2, LATS))] * 2
+    semaphores += [sems((2 + len(fixed),))]
+    in_vmem, anywhere = pl.BlockSpec(memory_space=pltpu.VMEM), pl.BlockSpec(memory_space=pl.ANY)
     return pl.pallas_call(
         kernel,
         out_shape=jax.ShapeDtypeStruct(light_field.shape, F32),
-        in_specs=[pl.BlockSpec(memory_space=pltpu.VMEM)] * 11,
+        in_specs=[anywhere] + [in_vmem] * 2 + [anywhere] + [in_vmem] * 3 + [anywhere] * len(fixed),
         out_specs=pl.BlockSpec(memory_space=pltpu.VMEM),
         scratch_shapes=exchange + tables + semaphores,
         compiler_params=pltpu.CompilerParams(
-            collective_id=0, has_side_effects=True, vmem_limit_bytes=50 * 1024 * 1024
+            collective_id=0, has_side_effects=True, vmem_limit_bytes=56 * 1024 * 1024
         ),
     )(
         light_field,
@@ -652,7 +722,7 @@
         bin_decay[None],
         bin_detune[None],
         group_bin[None],
-        *[jnp.asarray(c) for c in constants()],
+        *[jnp.asarray(c) for c in fixed],
     )
 
 

time: 73.2 us -> 71.3 us (0.974)
  local copies, waits for them, and re-layouts: 6.24 us -> 4.11 us
    unnamed x23 -> x5, local copies, waits for them, and re-layouts: 5.96 us -> 2.56 us
where the time goes in v2:
time: 71.3 us; the launch traced here: 71 us
  Pallas kernels  66.9 us (94%)
  local copies, waits for them, and re-layouts  4.11 us (6%)
    pallas_call x1, Pallas kernels, fused(): pl.pallas_call(kernel, out_shape=jax.ShapeDtypeStruct(light_field.shape,...  66.9 us
    unnamed x5, local copies, waits for them, and re-layouts  2.56 us

profile of v2, /device:TPU:0, one launch (start us, length us, event | category | flops | bytes accessed | tf_op | source)
XLA Modules:
  0.0 71.0 jit_solution(5126664130841610858)
XLA Ops:
  0.0 0.0 copy-start.1
  0.0 0.7 copy-done.1
  0.7 0.0 copy-start
  0.7 0.8 %reshape.6.latp = f32[256,4]{1,0:T(8,128)} reshape(f32[1024]{0:T(1024)S(1)} %copy-done.1) | data formatting | bytes 8192 | tf_op jit(solution)/shard_map/reshape | solution.py:719
  1.5 0.0 copy-done
  1.5 0.1 reshape.7
  1.6 0.7 copy.12
  2.2 66.9 %shard_map.109 = f32[2,256,256]{2,1,0:T(8,128)} custom-call(f32[2,256,256]{2,1,0:T(8,128)} %lf_hbm.1, f32[256,4]{1,0:T(8,128)} %reshape.6.latp, f32[8,256]{1,0:T(8,128)} %bitcast.4, f32[128,256]{1,0:T(8,128)} %occ_hbm.1, f32[1,32]{1,0:T(1,128)} %bitcast.5, f32[1,32]{1,0:T(1,128)} %bitcast.6, s32[1,128]{1,0:T(1,128)} %bitcast.7, ...), custom_call_target="tpu_custom_call" | custom-call | tf_op jit(solution)/shard_map/pallas_call | solution.py:708
  69.2 1.9 %copy.14 = f32[2,256,256]{2,1,0:T(8,128)} copy(f32[2,256,256]{2,1,0:T(8,128)} %shard_map.109) | data formatting | bytes 1048576
Async XLA Ops:
  0.0 0.7 copy-start.1
  0.7 0.8 %copy-start = (f32[2048]{0:T(1024)S(1)}, f32[2048]{0:T(1024)}, u32[]{:S(2)}) copy-start(f32[2048]{0:T(1024)} %param.13) | copy-start | bytes 24580

commit v3 on v2

--- a/solution.py
+++ b/solution.py
@@ -296,14 +296,48 @@
     return tiles
 
 
-def unpack(tiles):
-    first = lane_iota(tiles[0].shape) < 64
-    re, im = [], []
-    for p in range(0, len(tiles), 2):
-        a, b = tiles[p], tiles[p + 1]
-        re.append(jnp.where(first, a, roll(b, 64)))
-        im.append(jnp.where(first, roll(a, 64), b))
-    return jnp.concatenate(re, axis=1), jnp.concatenate(im, axis=1)
+def lane_part(shape):
+    return lane_iota(shape) // 32
+
+
+def pack_halves(re, im):
+    part = lane_part((re[0].shape[0], 128))
+    tiles = {}
+    for l in range(LATS):
+        for h in range(2):
+            at = 2 * (l % 2) + h
+            tile = None
+            for q, source in enumerate((re[0], re[1], im[0], im[1])):
+                piece = roll(source[:, 128 * (l // 2) : 128 * (l // 2) + 128], 32 * (q - at))
+                tile = piece if tile is None else jnp.where(part == q, piece, tile)
+            tiles[l, h] = tile
+    return tiles
+
+
+def unpack_halves(tiles):
+    part = lane_part(tiles[0, 0].shape)
+    done = []
+    for q in range(4):
+        joined = []
+        for p in range(LATS // 2):
+            value = None
+            for at in range(4):
+                piece = roll(tiles[2 * p + at // 2, at % 2], 32 * (at - q))
+                value = piece if value is None else jnp.where(part == at, piece, value)
+            joined.append(value)
+        done.append(jnp.concatenate(joined, axis=1))
+    return done[:2], done[2:]
+
+
+def join_rows(a, b):
+    count, width = a.shape
+    a, b = (x.reshape(count // PART, PART, width) for x in (a, b))
+    return jnp.stack([a, b], axis=1).reshape(2 * count, width)
+
+
+def part_rows(x):
+    x = x.reshape(x.shape[0] // ROWS, 2, PART, x.shape[1])
+    return tuple(x[:, i].reshape(-1, x.shape[-1]) for i in (0, 1))
 
 
 def turn(x):
@@ -315,8 +349,8 @@
 def kernel(
     lf_hbm, latp, specp, occ_hbm, dec_ref, det_ref, gb_ref, wh_hbm, wl_hbm, rows_hbm, cols_hbm,
     out,
-    s1, r1, s2, r2, s3a, r3a, s3b, r3b, s4, r4,
-    tw_c, tw_s, ph_c, ph_s, ct, q_hi, q_lo, p_hi, p_lo, kev, kod, kfe, kfo, spec,
+    s1, r1, s2, r2, s3a, r3a, s3b, r3b, s4a, r4a, s4b, r4b,
+    tw_c, tw_s, th_c, th_s, ph_c, ph_s, ct, q_hi, q_lo, p_hi, p_lo, kev, kod, kfe, kfo, spec,
     lf, occ, wh, wl, rows_ref, cols_ref,
     ss1, rs1, ss2, rs2, ss3, rs3, ss4, rs4, load_sem,
 ):
@@ -373,7 +407,7 @@
 
     def to_rows(h, d):
         t, tl, tm = other(d)
-        src = s2.at[tl, pl.ds(pl.multiple_of(tm * ROWS + h * PART, PART), PART)]
+        src = s2.at[h, tl, pl.ds(pl.multiple_of(tm * PART, PART), PART)]
         return remote(src, r2.at[h, m, l], ss2.at[h, t], rs2.at[h, me], tl, tm)
 
     def from_columns(h, d):
@@ -392,13 +426,17 @@
         return remote(here, here, ss3.at[h, t], rs3.at[h, t], tl, tm)
 
     loads[0].wait()
-    for t, tile in enumerate(pack(lf[0], lf[1])):
-        s1[t] = tile
+    for (t, h), tile in pack_halves(part_rows(lf[0]), part_rows(lf[1])).items():
+        s1[h, t] = tile
     pl.semaphore_wait(barrier, TOTAL - 1)
-    first = [lat_send(s1, r1, ss1, rs1, d) for d in range(1, LATS)]
-    for copy in first:
+    first = [
+        [lat_send(s1.at[h], r1.at[h], ss1.at[h], rs1.at[h], d) for d in range(1, LATS)]
+        for h in range(2)
+    ]
+    for copy in first[0]:
         copy.start()
-    r1[l] = s1[l]
+    for h in range(2):
+        r1[h, l] = s1[h, l]
 
     loads[1].wait()
     whole = (SIDE, 128)
@@ -406,11 +444,16 @@
     sign = jnp.where(lane_iota(whole) < 64, -1.0, 1.0)
     phase = latp[...]
     turn_c, turn_s = jnp.cos(phase) * (1.0 / WIDE), jnp.sin(phase) * (1.0 / WIDE)
+    second_set = lax.rem(lane_part((SIDE // 2, 128)), 2) == 1
+    second_key = lax.rem(lane_part(whole), 2) == 1
     for k in range(LATS):
         tw_c[k] = jnp.broadcast_to(cols_ref[:, k : k + 1], whole)
         tw_s[k] = jnp.broadcast_to(cols_ref[:, LATS + k : LATS + k + 1], whole) * sign
         ph_c[k] = jnp.broadcast_to(turn_c[:, k : k + 1], whole)
         ph_s[k] = jnp.broadcast_to(turn_s[:, k : k + 1], whole) * sign
+        for full, parted in ((tw_c, th_c), (tw_s, th_s)):
+            one, two = part_rows(full[k])
+            parted[k] = jnp.where(second_set, two, one)
 
     def wide_dft(re, im):
         x = halves(jnp.concatenate([re, im], axis=1))
@@ -427,7 +470,7 @@
         return tuple(jnp.concatenate([item[c] for item in items], axis=0) for c in (0, 1))
 
     def unstack(value):
-        return [tuple(v[PART * k : PART * (k + 1)] for v in value) for k in range(TIMES)]
+        return [tuple(v[ROWS * k : ROWS * (k + 1)] for v in value) for k in range(TIMES)]
 
     def time_dft(items):
         items = small_fft(items, -1)
@@ -452,20 +495,30 @@
             (y[:count, k : k + 128], y[count:, k : k + 128]) for k in range(0, x.shape[1], 128)
         ]
 
+    def butterfly(x, tables, back):
+        a, b, c, d = x[0] + x[2], x[0] - x[2], x[1] + x[3], turn(x[1] - x[3])
+        if back:
+            return [a + c, b + d, a - c, b - d]
+        across, along = tables
+        y = [a + c, b - d, a - c, b + d]
+        return [y[0]] + [y[k] * across[k] + roll(y[k], 64) * along[k] for k in (1, 2, 3)]
+
     def lateral_spectrum(x, states):
-        spectrum = []
-        for x in (x, states) if states else (x,):
-            a, b, c, d = x[0] + x[2], x[0] - x[2], x[1] + x[3], turn(x[1] - x[3])
-            for k, y in enumerate((a + c, b - d, a - c, b + d)):
-                spectrum.append(y * tw_c[k] + roll(y, 64) * tw_s[k] if k else y)
-        turns = [(ph_c[k], ph_s[k]) for k in range(LATS)]
+        y = butterfly(x, (th_c, th_s), False)
+        spectrum, turns = [], []
+        for k in (0, 2):
+            one = jnp.where(second_set, roll(y[k + 1], 32), y[k])
+            two = jnp.where(second_set, y[k + 1], roll(y[k], -32))
+            spectrum.append(join_rows(one, two))
+            turns.append(tuple(jnp.where(second_key, t[k + 1], t[k]) for t in (ph_c, ph_s)))
         if states:
-            tile, across, along = spectrum[LATS], turns[0][0], turns[0][1]
+            y = butterfly(states, (tw_c, tw_s), False)
+            tile, across, along = y[0], ph_c[0], ph_s[0]
             for k in range(1, LATS):
-                tile = jnp.where(group == k, roll(spectrum[LATS + k], 16 * k), tile)
-                across = jnp.where(group == k, turns[k][0], across)
-                along = jnp.where(group == k, turns[k][1], along)
-            spectrum[LATS:] = [tile]
+                tile = jnp.where(group == k, roll(y[k], 16 * k), tile)
+                across = jnp.where(group == k, ph_c[k], across)
+                along = jnp.where(group == k, ph_s[k], along)
+            spectrum.append(tile)
             turns.append((across, along))
         spectrum = column_dft(jnp.concatenate(spectrum, axis=1), 0, SIDE)
         done = []
@@ -474,33 +527,40 @@
             done.append(y * across + roll(y, 64) * along)
         return jnp.concatenate(done, axis=1)
 
+    def untwiddle(y, tables, low, high):
+        across, along = tables
+        for k in (1, 2, 3):
+            y[k] = y[k] * across[k, low:high, :] - roll(y[k], 64) * along[k, low:high, :]
+        return butterfly(y, None, True)
+
     def lateral_inverse(spectrum, low, high):
         result = [top + turn(bottom) for top, bottom in column_dft(spectrum, low, high)]
-        groups = [result[:LATS]]
-        if len(result) > LATS:
-            groups.append([roll(result[LATS], -16 * k) for k in range(LATS)])
-        done = []
-        for result in groups:
-            x = []
-            for k, y in enumerate(result):
-                if k:
-                    y = y * tw_c[k, low:high, :] - roll(y, 64) * tw_s[k, low:high, :]
-                x.append(y)
-            a, b, c, d = x[0] + x[2], x[0] - x[2], x[1] + x[3], turn(x[1] - x[3])
-            done.append([a + c, b + d, a - c, b - d])
+        mask = second_set[: (high - low) // 2]
+        y = []
+        for tile in result[:2]:
+            one, two = part_rows(tile)
+            y.append(jnp.where(mask, roll(two, 32), one))
+            y.append(jnp.where(mask, two, roll(one, -32)))
+        done = [untwiddle(y, (th_c, th_s), low // 2, high // 2)]
+        if len(result) > 2:
+            y = [roll(result[2], -16 * k) for k in range(LATS)]
+            done.append(untwiddle(y, (tw_c, tw_s), low, high))
         return done
 
     loads[2].wait()
     loads[3].wait()
-    for d in range(1, LATS):
-        lat_recv(s1, r1, ss1, rs1, d).wait_recv()
-    spectrum = lateral_spectrum([r1[a] for a in range(LATS)], None)
-    for a, tile in enumerate(lateral_inverse(spectrum, 0, SIDE)[0]):
-        s2[a] = tile
+    for copy in first[0]:
+        copy.wait_send()
+    for copy in first[1]:
+        copy.start()
     for h in range(2):
+        for d in range(1, LATS):
+            lat_recv(s1.at[h], r1.at[h], ss1.at[h], rs1.at[h], d).wait_recv()
+        spectrum = lateral_spectrum([r1[h, a] for a in range(LATS)], None)
+        for a, tile in enumerate(lateral_inverse(spectrum, 0, SIDE)[0]):
+            s2[h, a] = tile
         each(lambda d, h=h: to_rows(h, d).start())
-    for h in range(2):
-        r2[h, m, l] = s2[l, pl.ds(pl.multiple_of(m * ROWS + h * PART, PART), PART)]
+        r2[h, m, l] = s2[h, l, pl.ds(pl.multiple_of(m * PART, PART), PART)]
 
     loads[4].wait()
     loads[5].wait()
@@ -566,56 +626,55 @@
     far = []
     for k in range(TIMES):
         far.append(jnp.where(first_half, *power(float(SIDE * k), dec_lane, det_lane)))
+    mine = ct[pl.ds(pl.multiple_of(m * ROWS, ROWS), ROWS), :]
+    q = (q_hi[...], q_lo[...])
+    response = dot3(halves(jnp.concatenate([mine * f for f in far], axis=0)), q)
+    response = unstack((response[:, :SIDE], response[:, SIDE:]))
+    even = time_dft(response)
+    kev[0] = LONG * (1.0 - (0.5 * weight) * even[1])
+    kev[1] = (LONG * 0.5 * weight) * even[0]
+    odd = time_dft(twist(response, False))
+    kod[0] = (-0.5 * weight / LONG) * odd[1]
+    kod[1] = (0.5 * weight / LONG) * odd[0]
+
     for h in range(2):
-        mine = ct[pl.ds(pl.multiple_of(m * ROWS + h * PART, PART), PART), :]
-        q = (q_hi[...], q_lo[...])
-        response = jnp.concatenate([mine * f for f in far], axis=0)
-        response = dot3(halves(response), q)
-        response = unstack((response[:, :SIDE], response[:, SIDE:]))
-        even = time_dft(response)
-        kev[h, 0] = LONG * (1.0 - (0.5 * weight) * even[1])
-        kev[h, 1] = (LONG * 0.5 * weight) * even[0]
-        odd = time_dft(twist(response, False))
-        kod[h, 0] = (-0.5 * weight / LONG) * odd[1]
-        kod[h, 1] = (0.5 * weight / LONG) * odd[0]
-
+        each(lambda d, h=h: from_columns(h, d).wait_recv())
+    field = []
+    for k in range(TIMES):
+        re, im = unpack_halves({(a, h): r2[h, k, a] for a in range(LATS) for h in range(2)})
+        field.append((jnp.concatenate(re, axis=0), jnp.concatenate(im, axis=0)))
+    turn_row = stack([
+        tuple(jnp.broadcast_to(spec[c, k : k + 1, :], (ROWS, SIDE)) for c in (0, 1))
+        for k in range(TIMES)
+    ])
+    once = cmul(time_dft(field), turn_row)
+    twisted = time_dft(twist(time_inverse_dft(once), False))
+    twisted = time_inverse_dft(cmul(twisted, (kod[0], kod[1])))
+    late = time_dft(twist(twisted, True))
+    straight = cmul(once, (kev[0], kev[1]))
+    once = cmul((straight[0] + late[0], straight[1] + late[1]), turn_row)
+    field = time_inverse_dft(once)
+    flat = stack(field)
+    ends = dot3(halves(jnp.concatenate(flat, axis=1)), (p_hi[...], p_lo[...]))
+    ends = unstack((ends[:, :SIDE], ends[:, SIDE:]))
     step = power(float(SIDE), step_dec, step_det)
     slot = lax.rem(lane_iota((8, SIDE)) // 16, 4)
-    folded = [[jnp.zeros((8, SIDE), F32) for c in (0, 1)] for k in range(TIMES)]
-    for h in range(2):
-        each(lambda d, h=h: from_columns(h, d).wait_recv())
-        field = [unpack([r2[h, k, a] for a in range(LATS)]) for k in range(TIMES)]
-        turn_row = stack([
-            tuple(jnp.broadcast_to(spec[c, k : k + 1, :], (PART, SIDE)) for c in (0, 1))
-            for k in range(TIMES)
-        ])
-        once = cmul(time_dft(field), turn_row)
-        twisted = time_dft(twist(time_inverse_dft(once), False))
-        twisted = time_inverse_dft(cmul(twisted, (kod[h, 0], kod[h, 1])))
-        late = time_dft(twist(twisted, True))
-        straight = cmul(once, (kev[h, 0], kev[h, 1]))
-        once = cmul((straight[0] + late[0], straight[1] + late[1]), turn_row)
-        field = time_inverse_dft(once)
-        for k in range(TIMES):
-            for a, tile in enumerate(pack(*field[k])):
-                s3[h][k, a, :PART, :] = tile
-        if h == 0:
-            each(lambda d: to_columns(0, d).start())
-        flat = stack(field)
-        ends = dot3(halves(jnp.concatenate(flat, axis=1)), (p_hi[...], p_lo[...]))
-        ends = unstack((ends[:, :SIDE], ends[:, SIDE:]))
-        state = (jnp.zeros((PART, SIDE), F32), jnp.zeros((PART, SIDE), F32))
-        for k in range(TIMES):
-            for c in (0, 1):
-                for g in range(2):
-                    piece = state[c][8 * g : 8 * g + 8]
-                    folded[k][c] = jnp.where(slot == 2 * h + g, piece, folded[k][c])
-            moved = cmul(state, step)
-            state = (moved[0] + ends[k][0], moved[1] + ends[k][1])
+    state = (jnp.zeros((ROWS, SIDE), F32), jnp.zeros((ROWS, SIDE), F32))
     for k in range(TIMES):
-        for a, tile in enumerate(pack(*folded[k])):
-            s3b[k, a, PART:, :] = tile
-    each(lambda d: to_columns(1, d).start())
+        folded = []
+        for c in (0, 1):
+            total = state[c][:8]
+            for g in range(1, 4):
+                total = jnp.where(slot == g, state[c][8 * g : 8 * g + 8], total)
+            folded.append(total)
+        for a, tile in enumerate(pack(*folded)):
+            s3a[k, a, PART:, :] = tile
+        moved = cmul(state, step)
+        state = (moved[0] + ends[k][0], moved[1] + ends[k][1])
+        re, im = ((v[:PART], v[PART:]) for v in field[k])
+        for (a, h), tile in pack_halves(re, im).items():
+            s3[h][k, a, :PART, :] = tile
+    each(lambda d: to_columns(0, d).start())
     for h in range(2):
         r3[h][l, m] = s3[h][m, l]
 
@@ -628,45 +687,55 @@
     kfe[0], kfe[1] = -gain * even[1], gain * even[0]
     kfo[0], kfo[1] = -gain * odd[1], gain * odd[0]
 
-    for h in range(2):
-        each(lambda d, h=h: from_rows(h, d).wait_recv())
-    tiles, states = [], []
-    for a in range(LATS):
-        both = jnp.stack([r3a[a], r3b[a, :, :PART, :]], axis=1)
-        tiles.append(both.reshape(SIDE, 128))
-        extra = r3b[a, :, PART:, :].reshape(8 * TIMES, 128)
-        extra = [roll(extra, -16 * g).reshape(TIMES, 8, 128) for g in range(4)]
-        states.append(jnp.stack(extra, axis=1).reshape(SIDE, 128))
-    spectrum = lateral_spectrum(tiles, states)
+    each(lambda d: to_columns(0, d).wait_send())
+    each(lambda d: to_columns(1, d).start())
     span = SIDE // 2
     fold = span // 8
     slot = lax.rem(lane_iota((fold, 128)), 64) // 8
+    s4, r4 = (s4a, s4b), (r4a, r4b)
     last = []
     for h in range(2):
-        tiles, states = lateral_inverse(spectrum, span * h, span * (h + 1))
+        each(lambda d, h=h: from_rows(h, d).wait_recv())
+        tiles, states = [], []
         for a in range(LATS):
-            s4[h, a, :span, :] = tiles[a]
-            total = jnp.zeros((fold, 128), F32)
-            for g in range(8):
-                piece = roll(states[a][fold * g : fold * (g + 1)], 8 * g)
-                total = jnp.where(slot == g, piece, total)
-            s4[h, a, span:, :] = total
-        for d in range(1, LATS):
-            last.append(lat_send(s4.at[h], r4.at[h], ss4.at[h], rs4.at[h], d))
-            last[-1].start()
-        r4[h, l] = s4[h, l]
+            tiles.append(r3[h][a, :, :PART, :].reshape(span, 128))
+            if h == 0:
+                extra = r3a[a, :, PART:, :].reshape(8 * TIMES, 128)
+                extra = [roll(extra, -16 * g).reshape(TIMES, 8, 128) for g in range(4)]
+                states.append(jnp.stack(extra, axis=1).reshape(SIDE, 128))
+        spectrum = lateral_spectrum(tiles, states)
+        for u in range(2):
+            done = lateral_inverse(spectrum, span * u, span * (u + 1))
+            for a in range(LATS):
+                s4[h][u, a, : span // 2, :] = done[0][a]
+                if h == 0:
+                    total = done[1][a][:fold]
+                    for g in range(1, 8):
+                        piece = roll(done[1][a][fold * g : fold * (g + 1)], 8 * g)
+                        total = jnp.where(slot == g, piece, total)
+                    s4a[u, a, span // 2 :, :] = total
+            for d in range(1, LATS):
+                sems = ss4.at[h, u], rs4.at[h, u]
+                last.append(lat_send(s4[h].at[u], r4[h].at[u], *sems, d))
+                last[-1].start()
+            r4[h][u, l] = s4[h][u, l]
 
     slot = lax.rem(lane_iota((fold, 128)), 64) // 16
-    for h in range(2):
-        for d in range(1, LATS):
-            lat_recv(s4.at[h], r4.at[h], ss4.at[h], rs4.at[h], d).wait_recv()
-        here = pl.ds(span * h, span)
-        field = unpack([r4[h, a, :span, :] for a in range(LATS)])
+    for u in range(2):
+        for h in range(2):
+            for d in range(1, LATS):
+                sems = ss4.at[h, u], rs4.at[h, u]
+                lat_recv(s4[h].at[u], r4[h].at[u], *sems, d).wait_recv()
+        here = pl.ds(span * u, span)
+        re, im = unpack_halves({
+            (a, h): r4[h][u, a, : span // 2, :] for a in range(LATS) for h in range(2)
+        })
+        field = join_rows(*re), join_rows(*im)
         carried = []
         for g in range(8):
             total = jnp.zeros((fold, 128), F32)
             for a in range(LATS):
-                piece = roll(r4[h, a, span:, :], 16 * a - 8 * g)
+                piece = roll(r4a[u, a, span // 2 :, :], 16 * a - 8 * g)
                 total = jnp.where(slot == a, piece, total)
             carried.append(total)
         carried = halves(jnp.concatenate(carried, axis=0) * ct[here, :])
@@ -678,31 +747,33 @@
         out[0, here, :] = field[0] + even[0] + odd[0] - weight * carried[:, SIDE:]
         out[1, here, :] = field[1] + even[1] + odd[1] + weight * carried[:, :SIDE]
 
-    for copy in first + last:
+    for copy in first[1] + last:
         copy.wait_send()
     for h in range(2):
         each(lambda d, h=h: to_rows(h, d).wait_send())
-        each(lambda d, h=h: to_columns(h, d).wait_send())
+    each(lambda d: to_columns(1, d).wait_send())
 
 
 def fused(light_field, lateral_phase, spectral_phase, occupation, bin_decay, bin_detune, group_bin):
     tile = (SIDE, 128)
     vmem, sems = pltpu.VMEM, pltpu.SemaphoreType.DMA
     exchange = [
-        vmem((LATS,) + tile, F32), vmem((LATS,) + tile, F32),
-        vmem((LATS,) + tile, F32), vmem((2, TIMES, LATS, PART, 128), F32),
+        vmem((2, LATS, SIDE // 2, 128), F32), vmem((2, LATS, SIDE // 2, 128), F32),
+        vmem((2, LATS, SIDE // 2, 128), F32), vmem((2, TIMES, LATS, PART, 128), F32),
+        vmem((TIMES, LATS, PART + 8, 128), F32), vmem((LATS, TIMES, PART + 8, 128), F32),
         vmem((TIMES, LATS, PART, 128), F32), vmem((LATS, TIMES, PART, 128), F32),
-        vmem((TIMES, LATS, PART + 8, 128), F32), vmem((LATS, TIMES, PART + 8, 128), F32),
-        vmem((2, LATS, 9 * SIDE // 16, 128), F32), vmem((2, LATS, 9 * SIDE // 16, 128), F32),
+        vmem((2, LATS, 5 * SIDE // 16, 128), F32), vmem((2, LATS, 5 * SIDE // 16, 128), F32),
+        vmem((2, LATS, SIDE // 4, 128), F32), vmem((2, LATS, SIDE // 4, 128), F32),
     ]
-    tables = [vmem((LATS,) + tile, F32)] * 4 + [vmem(tile, F32)]
+    tables = [vmem((LATS,) + tile, F32)] * 2 + [vmem((LATS, SIDE // 2, 128), F32)] * 2
+    tables += [vmem((LATS,) + tile, F32)] * 2 + [vmem(tile, F32)]
     tables += [vmem((128, 2 * SIDE), BF16)] * 2 + [vmem((2 * SIDE, 2 * SIDE), BF16)] * 2
-    tables += [vmem((2, 2, SIDE // 2, SIDE), F32)] * 2 + [vmem((2, SIDE, SIDE), F32)] * 2
+    tables += [vmem((2, SIDE, SIDE), F32)] * 4
     tables += [vmem((2, TIMES, SIDE), F32)]
     fixed = constants()
     tables += [vmem(light_field.shape, F32), vmem(occupation.shape, F32)]
     tables += [vmem(c.shape, c.dtype) for c in fixed]
-    semaphores = [sems((LATS,))] * 2 + [sems((2, TOTAL))] * 4 + [sems((2, LATS))] * 2
+    semaphores = [sems((2, LATS))] * 2 + [sems((2, TOTAL))] * 4 + [sems((2, 2, LATS))] * 2
     semaphores += [sems((2 + len(fixed),))]
     in_vmem, anywhere = pl.BlockSpec(memory_space=pltpu.VMEM), pl.BlockSpec(memory_space=pl.ANY)
     return pl.pallas_call(

time: 71.3 us -> 69.7 us (0.978)
  Pallas kernels: 66.9 us -> 65.3 us
    pallas_call x1, Pallas kernels: 66.9 us -> 65.3 us  [fused(): pl.pallas_call(kernel, out_shape=jax.ShapeDtypeStruct(light_field.shape,...]
where the time goes in v3:
time: 69.7 us; the launch traced here: 69.5 us
  Pallas kernels  65.3 us (94%)
  local copies, waits for them, and re-layouts  4.11 us (6%)
    pallas_call x1, Pallas kernels, fused(): pl.pallas_call(kernel, out_shape=jax.ShapeDtypeStruct(light_field.shape,...  65.3 us
    unnamed x5, local copies, waits for them, and re-layouts  2.56 us

profile of v3, /device:TPU:0, one launch (start us, length us, event | category | flops | bytes accessed | tf_op | source)
XLA Modules:
  0.0 69.5 jit_solution(60531260026676322)
XLA Ops:
  0.0 0.0 copy-start.1
  0.0 0.7 copy-done.1
  0.7 0.0 copy-start
  0.7 0.8 %reshape.6.latp = f32[256,4]{1,0:T(8,128)} reshape(f32[1024]{0:T(1024)S(1)} %copy-done.1) | data formatting | bytes 8192 | tf_op jit(solution)/shard_map/reshape | solution.py:790
  1.5 0.0 copy-done
  1.5 0.1 reshape.7
  1.6 0.7 copy.12
  2.2 65.3 %shard_map.109 = f32[2,256,256]{2,1,0:T(8,128)} custom-call(f32[2,256,256]{2,1,0:T(8,128)} %lf_hbm.1, f32[256,4]{1,0:T(8,128)} %reshape.6.latp, f32[8,256]{1,0:T(8,128)} %bitcast.4, f32[128,256]{1,0:T(8,128)} %occ_hbm.1, f32[1,32]{1,0:T(1,128)} %bitcast.5, f32[1,32]{1,0:T(1,128)} %bitcast.6, s32[1,128]{1,0:T(1,128)} %bitcast.7, ...), custom_call_target="tpu_custom_call" | custom-call | tf_op jit(solution)/shard_map/pallas_call | solution.py:779
  67.6 1.9 %copy.14 = f32[2,256,256]{2,1,0:T(8,128)} copy(f32[2,256,256]{2,1,0:T(8,128)} %shard_map.109) | data formatting | bytes 1048576
Async XLA Ops:
  0.0 0.7 copy-start.1
  0.7 0.8 %copy-start = (f32[2048]{0:T(1024)S(1)}, f32[2048]{0:T(1024)}, u32[]{:S(2)}) copy-start(f32[2048]{0:T(1024)} %param.13) | copy-start | bytes 24580

commit v4 on v3

--- a/solution.py
+++ b/solution.py
@@ -228,7 +228,8 @@
     tw8 = np.exp(-2j * np.pi * np.outer(np.arange(TIMES), j) / LONG)
     tau = np.exp(-1j * np.pi * np.arange(LONG).reshape(TIMES, SIDE) / LONG)
     tau2 = np.exp(-1j * np.pi * j / SIDE)[None]
-    rows = np.concatenate([tw8, tau, tau2, np.zeros((7, SIDE))])
+    ones = np.ones((TIMES, SIDE))
+    rows = np.concatenate([tw8, tau, tau.conj(), ones, tau2, ones[1:]])
     rows = np.stack([rows.real, rows.imag]).astype(np.float32)
     tw4 = np.exp(-2j * np.pi * np.outer(j, np.arange(LATS)) / WIDE)
     cols = np.concatenate([tw4.real, tw4.imag], axis=1).astype(np.float32)
@@ -350,7 +351,7 @@
     lf_hbm, latp, specp, occ_hbm, dec_ref, det_ref, gb_ref, wh_hbm, wl_hbm, rows_hbm, cols_hbm,
     out,
     s1, r1, s2, r2, s3a, r3a, s3b, r3b, s4a, r4a, s4b, r4b,
-    tw_c, tw_s, th_c, th_s, ph_c, ph_s, ct, q_hi, q_lo, p_hi, p_lo, kev, kod, kfe, kfo, spec,
+    tw_c, tw_s, th_c, th_s, ph_c, ph_s, ct, q_hi, q_lo, p_hi, p_lo, mul, add, kf, xb, yb, kept, spec,
     lf, occ, wh, wl, rows_ref, cols_ref,
     ss1, rs1, ss2, rs2, ss3, rs3, ss4, rs4, load_sem,
 ):
@@ -463,34 +464,49 @@
     def wide_inverse(re, im):
         return conj(wide_dft(re, -im))
 
-    def row(k):
-        return rows_ref[0, k : k + 1, :], rows_ref[1, k : k + 1, :]
-
-    def stack(items):
-        return tuple(jnp.concatenate([item[c] for item in items], axis=0) for c in (0, 1))
-
-    def unstack(value):
-        return [tuple(v[ROWS * k : ROWS * (k + 1)] for v in value) for k in range(TIMES)]
-
-    def time_dft(items):
-        items = small_fft(items, -1)
-        return wide_dft(*stack([cmul(item, row(k)) for k, item in enumerate(items)]))
-
-    def time_inverse_dft(value):
-        items = unstack(wide_inverse(*value))
-        return small_fft([cmul(item, conj(row(k))) for k, item in enumerate(items)], 1)
-
-    def twist(items, back):
-        rows = [row(TIMES + k) for k in range(TIMES)]
-        return [cmul(x, conj(r) if back else r) for x, r in zip(items, rows)]
-
-    def column_dft(x, low, high):
+    def block(i):
+        at = pl.ds(pl.multiple_of(8 * i, 8), 8)
+        return rows_ref[0, at, :], rows_ref[1, at, :]
+
+    def row(table, k):
+        return table[0][k : k + 1], table[1][k : k + 1]
+
+    def groups_of_rows(body):
+        def step(g, carry):
+            body([pl.ds(pl.multiple_of(ROWS * k + 8 * g, 8), 8) for k in range(TIMES)])
+            return carry
+
+        lax.fori_loop(0, ROWS // 8, step, 0)
+
+    def time_dft(src, pre=None):
+        def body(spots):
+            items = [(src[0, at, :], src[1, at, :]) for at in spots]
+            if pre is not None:
+                items = [cmul(x, row(pre, k)) for k, x in enumerate(items)]
+            items = small_fft(items, -1)
+            for k, at in enumerate(spots):
+                yb[0, at, :], yb[1, at, :] = cmul(items[k], row(block(0), k))
+
+        groups_of_rows(body)
+        return wide_dft(yb[0], yb[1])
+
+    def time_inverse_dft(value, post):
+        yb[0], yb[1] = wide_inverse(*value)
+
+        def body(spots):
+            items = [(yb[0, at, :], yb[1, at, :]) for at in spots]
+            items = [cmul(x, conj(row(block(0), k))) for k, x in enumerate(items)]
+            for k, x in enumerate(small_fft(items, 1)):
+                xb[0, spots[k], :], xb[1, spots[k], :] = cmul(x, row(post, k))
+
+        groups_of_rows(body)
+
+    def column_dft(x, low, count):
         w = [
-            jnp.concatenate([ref[low:high, :SIDE], ref[SIDE + low : SIDE + high, :SIDE]], axis=0)
+            jnp.concatenate([ref[pl.ds(at, count), :SIDE] for at in (low, SIDE + low)], axis=0)
             for ref in (wh, wl)
         ]
         y = dot3(w, halves(x))
-        count = high - low
         return [
             (y[:count, k : k + 128], y[count:, k : k + 128]) for k in range(0, x.shape[1], 128)
         ]
@@ -527,24 +543,25 @@
             done.append(y * across + roll(y, 64) * along)
         return jnp.concatenate(done, axis=1)
 
-    def untwiddle(y, tables, low, high):
+    def untwiddle(y, tables, low, count):
         across, along = tables
+        here = pl.ds(low, count)
         for k in (1, 2, 3):
-            y[k] = y[k] * across[k, low:high, :] - roll(y[k], 64) * along[k, low:high, :]
+            y[k] = y[k] * across[k, here, :] - roll(y[k], 64) * along[k, here, :]
         return butterfly(y, None, True)
 
-    def lateral_inverse(spectrum, low, high):
-        result = [top + turn(bottom) for top, bottom in column_dft(spectrum, low, high)]
-        mask = second_set[: (high - low) // 2]
+    def lateral_inverse(spectrum, low, half_low, count):
+        result = [top + turn(bottom) for top, bottom in column_dft(spectrum, low, count)]
+        mask = second_set[: count // 2]
         y = []
         for tile in result[:2]:
             one, two = part_rows(tile)
             y.append(jnp.where(mask, roll(two, 32), one))
             y.append(jnp.where(mask, two, roll(one, -32)))
-        done = [untwiddle(y, (th_c, th_s), low // 2, high // 2)]
+        done = [untwiddle(y, (th_c, th_s), half_low, count // 2)]
         if len(result) > 2:
             y = [roll(result[2], -16 * k) for k in range(LATS)]
-            done.append(untwiddle(y, (tw_c, tw_s), low, high))
+            done.append(untwiddle(y, (tw_c, tw_s), low, count))
         return done
 
     loads[2].wait()
@@ -553,14 +570,18 @@
         copy.wait_send()
     for copy in first[1]:
         copy.start()
-    for h in range(2):
+
+    def column_half(h, carry):
         for d in range(1, LATS):
             lat_recv(s1.at[h], r1.at[h], ss1.at[h], rs1.at[h], d).wait_recv()
         spectrum = lateral_spectrum([r1[h, a] for a in range(LATS)], None)
-        for a, tile in enumerate(lateral_inverse(spectrum, 0, SIDE)[0]):
+        for a, tile in enumerate(lateral_inverse(spectrum, 0, 0, SIDE)[0]):
             s2[h, a] = tile
-        each(lambda d, h=h: to_rows(h, d).start())
+        each(lambda d: to_rows(h, d).start())
         r2[h, m, l] = s2[h, l, pl.ds(pl.multiple_of(m * PART, PART), PART)]
+        return carry
+
+    lax.fori_loop(0, 2, column_half, 0)
 
     loads[4].wait()
     loads[5].wait()
@@ -629,38 +650,61 @@
     mine = ct[pl.ds(pl.multiple_of(m * ROWS, ROWS), ROWS), :]
     q = (q_hi[...], q_lo[...])
     response = dot3(halves(jnp.concatenate([mine * f for f in far], axis=0)), q)
-    response = unstack((response[:, :SIDE], response[:, SIDE:]))
-    even = time_dft(response)
-    kev[0] = LONG * (1.0 - (0.5 * weight) * even[1])
-    kev[1] = (LONG * 0.5 * weight) * even[0]
-    odd = time_dft(twist(response, False))
-    kod[0] = (-0.5 * weight / LONG) * odd[1]
-    kod[1] = (0.5 * weight / LONG) * odd[0]
+    xb[0], xb[1] = response[:, :SIDE], response[:, SIDE:]
+
+    def spectra(e, carry):
+        mul[e, 0], mul[e, 1] = time_dft(xb, block(3 - 2 * e))
+        return carry
+
+    lax.fori_loop(0, 2, spectra, 0)
+    gain = 0.5 * weight
+    even = 1.0 - gain * mul[0, 1], gain * mul[0, 0]
+    odd = (-gain / LONG) * mul[1, 1], (gain / LONG) * mul[1, 0]
+    turn_row = tuple(
+        jnp.concatenate(
+            [jnp.broadcast_to(spec[c, k : k + 1, :], (ROWS, SIDE)) for k in range(TIMES)], axis=0
+        )
+        for c in (0, 1)
+    )
+    even = cmul(even, turn_row)
+    for c in (0, 1):
+        mul[0, c], mul[1, c], mul[2, c] = turn_row[c], odd[c], turn_row[c]
+        add[0, c], add[1, c] = jnp.zeros((SIDE, SIDE), F32), jnp.zeros((SIDE, SIDE), F32)
+        add[2, c] = LONG * even[c]
+        kept[c] = jnp.zeros((SIDE, SIDE), F32)
 
     for h in range(2):
         each(lambda d, h=h: from_columns(h, d).wait_recv())
-    field = []
-    for k in range(TIMES):
+
+    def gather(k, carry):
         re, im = unpack_halves({(a, h): r2[h, k, a] for a in range(LATS) for h in range(2)})
-        field.append((jnp.concatenate(re, axis=0), jnp.concatenate(im, axis=0)))
-    turn_row = stack([
-        tuple(jnp.broadcast_to(spec[c, k : k + 1, :], (ROWS, SIDE)) for c in (0, 1))
-        for k in range(TIMES)
-    ])
-    once = cmul(time_dft(field), turn_row)
-    twisted = time_dft(twist(time_inverse_dft(once), False))
-    twisted = time_inverse_dft(cmul(twisted, (kod[0], kod[1])))
-    late = time_dft(twist(twisted, True))
-    straight = cmul(once, (kev[0], kev[1]))
-    once = cmul((straight[0] + late[0], straight[1] + late[1]), turn_row)
-    field = time_inverse_dft(once)
-    flat = stack(field)
-    ends = dot3(halves(jnp.concatenate(flat, axis=1)), (p_hi[...], p_lo[...]))
-    ends = unstack((ends[:, :SIDE], ends[:, SIDE:]))
+        at = pl.ds(pl.multiple_of(ROWS * k, ROWS), ROWS)
+        xb[0, at, :] = jnp.concatenate(re, axis=0)
+        xb[1, at, :] = jnp.concatenate(im, axis=0)
+        return carry
+
+    lax.fori_loop(0, TIMES, gather, 0)
+
+    def advance(i, carry):
+        y = cmul(time_dft(xb), (mul[i, 0], mul[i, 1]))
+        z = cmul((kept[0], kept[1]), (add[i, 0], add[i, 1]))
+        y = y[0] + z[0], y[1] + z[1]
+
+        @pl.when(i == 0)
+        def keep():
+            kept[0], kept[1] = y
+
+        time_inverse_dft(y, block(1 + i))
+        return carry
+
+    lax.fori_loop(0, 3, advance, 0)
+    flat = jnp.concatenate([xb[0], xb[1]], axis=1)
+    ends = dot3(halves(flat), (p_hi[...], p_lo[...]))
+    yb[0], yb[1] = ends[:, :SIDE], ends[:, SIDE:]
     step = power(float(SIDE), step_dec, step_det)
     slot = lax.rem(lane_iota((8, SIDE)) // 16, 4)
-    state = (jnp.zeros((ROWS, SIDE), F32), jnp.zeros((ROWS, SIDE), F32))
-    for k in range(TIMES):
+
+    def hand_out(k, state):
         folded = []
         for c in (0, 1):
             total = state[c][:8]
@@ -669,23 +713,29 @@
             folded.append(total)
         for a, tile in enumerate(pack(*folded)):
             s3a[k, a, PART:, :] = tile
+        at = pl.ds(pl.multiple_of(ROWS * k, ROWS), ROWS)
         moved = cmul(state, step)
-        state = (moved[0] + ends[k][0], moved[1] + ends[k][1])
-        re, im = ((v[:PART], v[PART:]) for v in field[k])
+        re, im = ((v[:PART], v[PART:]) for v in (xb[0, at, :], xb[1, at, :]))
         for (a, h), tile in pack_halves(re, im).items():
             s3[h][k, a, :PART, :] = tile
+        return (moved[0] + yb[0, at, :], moved[1] + yb[1, at, :])
+
+    zero = jnp.zeros((ROWS, SIDE), F32)
+    lax.fori_loop(0, TIMES, hand_out, (zero, zero))
     each(lambda d: to_columns(0, d).start())
     for h in range(2):
         r3[h][l, m] = s3[h][m, l]
 
-    t2 = rows_ref[0, 2 * TIMES : 2 * TIMES + 1, :], rows_ref[1, 2 * TIMES : 2 * TIMES + 1, :]
     q = (q_hi[...], q_lo[...])
     response = dot3(halves(jnp.where(lane_iota(whole) < 64, ct[...], 0.0)), q)
-    response = (response[:, :SIDE], response[:, SIDE:])
-    even, odd = wide_dft(*response), wide_dft(*cmul(response, t2))
-    gain = 0.5 * weight / SIDE
-    kfe[0], kfe[1] = -gain * even[1], gain * even[0]
-    kfo[0], kfo[1] = -gain * odd[1], gain * odd[0]
+    yb[0], yb[1] = response[:, :SIDE], response[:, SIDE:]
+
+    def own_spectra(e, carry):
+        re, im = wide_dft(*cmul((yb[0], yb[1]), row(block(3 + e), 0)))
+        kf[e, 0], kf[e, 1] = (-gain / SIDE) * im, (gain / SIDE) * re
+        return carry
+
+    lax.fori_loop(0, 2, own_spectra, 0)
 
     each(lambda d: to_columns(0, d).wait_send())
     each(lambda d: to_columns(1, d).start())
@@ -693,7 +743,6 @@
     fold = span // 8
     slot = lax.rem(lane_iota((fold, 128)), 64) // 8
     s4, r4 = (s4a, s4b), (r4a, r4b)
-    last = []
     for h in range(2):
         each(lambda d, h=h: from_rows(h, d).wait_recv())
         tiles, states = [], []
@@ -704,8 +753,10 @@
                 extra = [roll(extra, -16 * g).reshape(TIMES, 8, 128) for g in range(4)]
                 states.append(jnp.stack(extra, axis=1).reshape(SIDE, 128))
         spectrum = lateral_spectrum(tiles, states)
-        for u in range(2):
-            done = lateral_inverse(spectrum, span * u, span * (u + 1))
+
+        def send_part(u, carry, h=h, spectrum=spectrum):
+            low = pl.multiple_of(span * u, span)
+            done = lateral_inverse(spectrum, low, pl.multiple_of(low // 2, span // 2), span)
             for a in range(LATS):
                 s4[h][u, a, : span // 2, :] = done[0][a]
                 if h == 0:
@@ -716,17 +767,20 @@
                     s4a[u, a, span // 2 :, :] = total
             for d in range(1, LATS):
                 sems = ss4.at[h, u], rs4.at[h, u]
-                last.append(lat_send(s4[h].at[u], r4[h].at[u], *sems, d))
-                last[-1].start()
+                lat_send(s4[h].at[u], r4[h].at[u], *sems, d).start()
             r4[h][u, l] = s4[h][u, l]
-
-    slot = lax.rem(lane_iota((fold, 128)), 64) // 16
-    for u in range(2):
+            return carry
+
+        lax.fori_loop(0, 2, send_part, 0)
+
+    slot4 = lax.rem(lane_iota((fold, 128)), 64) // 16
+
+    def finish(u, carry):
         for h in range(2):
             for d in range(1, LATS):
                 sems = ss4.at[h, u], rs4.at[h, u]
                 lat_recv(s4[h].at[u], r4[h].at[u], *sems, d).wait_recv()
-        here = pl.ds(span * u, span)
+        here = pl.ds(pl.multiple_of(span * u, span), span)
         re, im = unpack_halves({
             (a, h): r4[h][u, a, : span // 2, :] for a in range(LATS) for h in range(2)
         })
@@ -736,19 +790,34 @@
             total = jnp.zeros((fold, 128), F32)
             for a in range(LATS):
                 piece = roll(r4a[u, a, span // 2 :, :], 16 * a - 8 * g)
-                total = jnp.where(slot == a, piece, total)
+                total = jnp.where(slot4 == a, piece, total)
             carried.append(total)
         carried = halves(jnp.concatenate(carried, axis=0) * ct[here, :])
         carried = dot3(carried, (q_hi[...], q_lo[...]))
-        even = wide_inverse(*cmul(wide_dft(*field), (kfe[0, here, :], kfe[1, here, :])))
-        odd = wide_dft(*cmul(field, t2))
-        odd = wide_inverse(*cmul(odd, (kfo[0, here, :], kfo[1, here, :])))
-        odd = cmul(odd, conj(t2))
-        out[0, here, :] = field[0] + even[0] + odd[0] - weight * carried[:, SIDE:]
-        out[1, here, :] = field[1] + even[1] + odd[1] + weight * carried[:, :SIDE]
-
-    for copy in first[1] + last:
+        out[0, here, :] = field[0] - weight * carried[:, SIDE:]
+        out[1, here, :] = field[1] + weight * carried[:, :SIDE]
+
+        def add_part(e, inner):
+            twist = row(block(3 + e), 0)
+            y = wide_dft(*cmul(field, twist))
+            y = wide_inverse(*cmul(y, (kf[e, 0, here, :], kf[e, 1, here, :])))
+            y = cmul(y, conj(twist))
+            for c in (0, 1):
+                out[c, here, :] = out[c, here, :] + y[c]
+            return inner
+
+        lax.fori_loop(0, 2, add_part, 0)
+        return carry
+
+    lax.fori_loop(0, 2, finish, 0)
+
+    for copy in first[1]:
         copy.wait_send()
+    for h in range(2):
+        for u in range(2):
+            for d in range(1, LATS):
+                sems = ss4.at[h, u], rs4.at[h, u]
+                lat_send(s4[h].at[u], r4[h].at[u], *sems, d).wait_send()
     for h in range(2):
         each(lambda d, h=h: to_rows(h, d).wait_send())
     each(lambda d: to_columns(1, d).wait_send())
@@ -768,7 +837,8 @@
     tables = [vmem((LATS,) + tile, F32)] * 2 + [vmem((LATS, SIDE // 2, 128), F32)] * 2
     tables += [vmem((LATS,) + tile, F32)] * 2 + [vmem(tile, F32)]
     tables += [vmem((128, 2 * SIDE), BF16)] * 2 + [vmem((2 * SIDE, 2 * SIDE), BF16)] * 2
-    tables += [vmem((2, SIDE, SIDE), F32)] * 4
+    tables += [vmem((3, 2, SIDE, SIDE), F32)] * 2 + [vmem((2, 2, SIDE, SIDE), F32)]
+    tables += [vmem((2, SIDE, SIDE), F32)] * 3
     tables += [vmem((2, TIMES, SIDE), F32)]
     fixed = constants()
     tables += [vmem(light_field.shape, F32), vmem(occupation.shape, F32)]

time: 69.7 us -> 72.5 us (1.040)
  Pallas kernels: 65.3 us -> 68.2 us
    pallas_call x1, Pallas kernels: 65.3 us -> 68.2 us  [fused(): pl.pallas_call(kernel, out_shape=jax.ShapeDtypeStruct(light_field.shape,...]
where the time goes in v4:
time: 72.5 us; the launch traced here: 72.3 us
  Pallas kernels  68.2 us (94%)
  local copies, waits for them, and re-layouts  4.11 us (6%)
    pallas_call x1, Pallas kernels, fused(): pl.pallas_call(kernel, out_shape=jax.ShapeDtypeStruct(light_field.shape,...  68.2 us
    unnamed x5, local copies, waits for them, and re-layouts  2.56 us

profile of v4, /device:TPU:0, one launch (start us, length us, event | category | flops | bytes accessed | tf_op | source)
XLA Modules:
  0.0 72.3 jit_solution(17989226859695414376)
XLA Ops:
  0.0 0.0 copy-start.1
  0.0 0.7 copy-done.1
  0.7 0.0 copy-start
  0.7 0.8 %reshape.6.latp = f32[256,4]{1,0:T(8,128)} reshape(f32[1024]{0:T(1024)S(1)} %copy-done.1) | data formatting | bytes 8192 | tf_op jit(solution)/shard_map/reshape | solution.py:860
  1.5 0.0 copy-done
  1.5 0.1 reshape.7
  1.6 0.7 copy.12
  2.2 68.2 %shard_map.109 = f32[2,256,256]{2,1,0:T(8,128)} custom-call(f32[2,256,256]{2,1,0:T(8,128)} %lf_hbm.1, f32[256,4]{1,0:T(8,128)} %reshape.6.latp, f32[8,256]{1,0:T(8,128)} %bitcast.4, f32[128,256]{1,0:T(8,128)} %occ_hbm.1, f32[1,32]{1,0:T(1,128)} %bitcast.5, f32[1,32]{1,0:T(1,128)} %bitcast.6, s32[1,128]{1,0:T(1,128)} %bitcast.7, ...), custom_call_target="tpu_custom_call" | custom-call | tf_op jit(solution)/shard_map/pallas_call | solution.py:849
  70.4 1.9 %copy.14 = f32[2,256,256]{2,1,0:T(8,128)} copy(f32[2,256,256]{2,1,0:T(8,128)} %shard_map.109) | data formatting | bytes 1048576
Async XLA Ops:
  0.0 0.7 copy-start.1
  0.7 0.8 %copy-start = (f32[2048]{0:T(1024)S(1)}, f32[2048]{0:T(1024)}, u32[]{:S(2)}) copy-start(f32[2048]{0:T(1024)} %param.13) | copy-start | bytes 24580

commit v5 on v3

--- a/solution.py
+++ b/solution.py
@@ -362,31 +362,28 @@
         loads.append(pltpu.make_async_copy(src, dst, load_sem.at[i]))
         loads[-1].start()
     l, m = lax.axis_index("lat"), lax.axis_index("tm")
-    me = l * TIMES + m
     weight = GAIN_SCALE / math.sqrt(occ.shape[0])
 
     half = TIMES // 2
 
-    def other(d):
-        side = lax.rem(m // half + 1 + d // (TOTAL // 2), 2)
-        tm = side * half + lax.rem(m + d, half)
-        tl = lax.rem(l + lax.rem(d // half, LATS), LATS)
-        return tl * TIMES + tm, tl, tm
+    lats = [l] + [lax.rem(l + d, LATS) for d in range(1, LATS)]
+    side = m // half
+    sides = [lax.rem(side + 1, 2) * half, side * half]
+    steps = [lax.rem(m + d, half) for d in range(half)]
+    times = [[sides[i] + step for step in steps] for i in (0, 1)]
+    others = []
+    for d in range(TOTAL // 2):
+        for i in (0, 1):
+            if i == 0 or d:
+                others.append((lats[d // half], times[i][d % half]))
 
     def each(act):
-        act(0)
-
-        def body(d, carry):
-            act(d)
-            act(d + TOTAL // 2)
-            return carry
-
-        lax.fori_loop(1, TOTAL // 2, body, 0)
+        for tl, tm in others:
+            act(tl, tm)
 
     barrier = pltpu.get_barrier_semaphore()
 
-    def greet(d):
-        t, tl, tm = other(d)
+    def greet(tl, tm):
         pl.semaphore_signal(barrier, inc=1, device_id=(tl, tm), device_id_type=MESH)
 
     each(greet)
@@ -398,32 +395,27 @@
         )
 
     def lat_send(s, r, ss, rs, d):
-        t = lax.rem(l + d, LATS)
-        return remote(s.at[t], r.at[l], ss.at[t], rs.at[l], t, m)
-
-    def lat_recv(s, r, ss, rs, d):
-        t = lax.rem(l + d, LATS)
-        return remote(s.at[t], r.at[t], ss.at[t], rs.at[t], t, m)
-
-    def to_rows(h, d):
-        t, tl, tm = other(d)
+        return remote(s.at[lats[d]], r.at[l], ss, rs, lats[d], m)
+
+    def all_of(ref, count, ss, rs):
+        part = ref.at[pl.ds(0, count)]
+        return remote(part, part, ss, rs, lats[1], m)
+
+    s3, r3 = (s3a, s3b), (r3a, r3b)
+
+    def to_rows(h, tl, tm):
         src = s2.at[h, tl, pl.ds(pl.multiple_of(tm * PART, PART), PART)]
-        return remote(src, r2.at[h, m, l], ss2.at[h, t], rs2.at[h, me], tl, tm)
-
-    def from_columns(h, d):
-        t, tl, tm = other(d)
-        return remote(r2.at[h, tm, tl], r2.at[h, tm, tl], ss2.at[h, t], rs2.at[h, t], tl, tm)
-
-    s3, r3 = (s3a, s3b), (r3a, r3b)
-
-    def to_columns(h, d):
-        t, tl, tm = other(d)
-        return remote(s3[h].at[tm, tl], r3[h].at[l, m], ss3.at[h, t], rs3.at[h, me], tl, tm)
-
-    def from_rows(h, d):
-        t, tl, tm = other(d)
-        here = r3[h].at[tl, tm]
-        return remote(here, here, ss3.at[h, t], rs3.at[h, t], tl, tm)
+        return remote(src, r2.at[h, m * LATS + l], ss2.at[h], rs2.at[h], tl, tm)
+
+    def to_columns(h, tl, tm):
+        dst = r3[h].at[l * TIMES + m]
+        return remote(s3[h].at[tm * LATS + tl], dst, ss3.at[h], rs3.at[h], tl, tm)
+
+    def rows_all(h):
+        return all_of(r2.at[h], TOTAL - 1, ss2.at[h], rs2.at[h])
+
+    def columns_all(h):
+        return all_of(r3[h], TOTAL - 1, ss3.at[h], rs3.at[h])
 
     loads[0].wait()
     for (t, h), tile in pack_halves(part_rows(lf[0]), part_rows(lf[1])).items():
@@ -549,18 +541,19 @@
 
     loads[2].wait()
     loads[3].wait()
-    for copy in first[0]:
-        copy.wait_send()
+    def first_all(h):
+        return all_of(r1.at[h], LATS - 1, ss1.at[h], rs1.at[h])
+
+    first_all(0).wait_send()
     for copy in first[1]:
         copy.start()
     for h in range(2):
-        for d in range(1, LATS):
-            lat_recv(s1.at[h], r1.at[h], ss1.at[h], rs1.at[h], d).wait_recv()
+        first_all(h).wait_recv()
         spectrum = lateral_spectrum([r1[h, a] for a in range(LATS)], None)
         for a, tile in enumerate(lateral_inverse(spectrum, 0, SIDE)[0]):
             s2[h, a] = tile
-        each(lambda d, h=h: to_rows(h, d).start())
-        r2[h, m, l] = s2[h, l, pl.ds(pl.multiple_of(m * PART, PART), PART)]
+        each(lambda tl, tm, h=h: to_rows(h, tl, tm).start())
+        r2[h, m * LATS + l] = s2[h, l, pl.ds(pl.multiple_of(m * PART, PART), PART)]
 
     loads[4].wait()
     loads[5].wait()
@@ -638,10 +631,10 @@
     kod[1] = (0.5 * weight / LONG) * odd[0]
 
     for h in range(2):
-        each(lambda d, h=h: from_columns(h, d).wait_recv())
+        rows_all(h).wait_recv()
     field = []
     for k in range(TIMES):
-        re, im = unpack_halves({(a, h): r2[h, k, a] for a in range(LATS) for h in range(2)})
+        re, im = unpack_halves({(a, h): r2[h, k * LATS + a] for a in range(LATS) for h in range(2)})
         field.append((jnp.concatenate(re, axis=0), jnp.concatenate(im, axis=0)))
     turn_row = stack([
         tuple(jnp.broadcast_to(spec[c, k : k + 1, :], (ROWS, SIDE)) for c in (0, 1))
@@ -668,15 +661,15 @@
                 total = jnp.where(slot == g, state[c][8 * g : 8 * g + 8], total)
             folded.append(total)
         for a, tile in enumerate(pack(*folded)):
-            s3a[k, a, PART:, :] = tile
+            s3a[k * LATS + a, PART:, :] = tile
         moved = cmul(state, step)
         state = (moved[0] + ends[k][0], moved[1] + ends[k][1])
         re, im = ((v[:PART], v[PART:]) for v in field[k])
         for (a, h), tile in pack_halves(re, im).items():
-            s3[h][k, a, :PART, :] = tile
-    each(lambda d: to_columns(0, d).start())
+            s3[h][k * LATS + a, :PART, :] = tile
+    each(lambda tl, tm: to_columns(0, tl, tm).start())
     for h in range(2):
-        r3[h][l, m] = s3[h][m, l]
+        r3[h][l * TIMES + m] = s3[h][m * LATS + l]
 
     t2 = rows_ref[0, 2 * TIMES : 2 * TIMES + 1, :], rows_ref[1, 2 * TIMES : 2 * TIMES + 1, :]
     q = (q_hi[...], q_lo[...])
@@ -687,20 +680,24 @@
     kfe[0], kfe[1] = -gain * even[1], gain * even[0]
     kfo[0], kfo[1] = -gain * odd[1], gain * odd[0]
 
-    each(lambda d: to_columns(0, d).wait_send())
-    each(lambda d: to_columns(1, d).start())
+    columns_all(0).wait_send()
+    each(lambda tl, tm: to_columns(1, tl, tm).start())
     span = SIDE // 2
     fold = span // 8
     slot = lax.rem(lane_iota((fold, 128)), 64) // 8
     s4, r4 = (s4a, s4b), (r4a, r4b)
-    last = []
+
+    def last_all(h, u):
+        return all_of(r4[h].at[u], LATS - 1, ss4.at[h, u], rs4.at[h, u])
+
     for h in range(2):
-        each(lambda d, h=h: from_rows(h, d).wait_recv())
+        columns_all(h).wait_recv()
         tiles, states = [], []
         for a in range(LATS):
-            tiles.append(r3[h][a, :, :PART, :].reshape(span, 128))
+            mine = slice(a * TIMES, (a + 1) * TIMES)
+            tiles.append(r3[h][mine, :PART, :].reshape(span, 128))
             if h == 0:
-                extra = r3a[a, :, PART:, :].reshape(8 * TIMES, 128)
+                extra = r3a[mine, PART:, :].reshape(8 * TIMES, 128)
                 extra = [roll(extra, -16 * g).reshape(TIMES, 8, 128) for g in range(4)]
                 states.append(jnp.stack(extra, axis=1).reshape(SIDE, 128))
         spectrum = lateral_spectrum(tiles, states)
@@ -716,16 +713,13 @@
                     s4a[u, a, span // 2 :, :] = total
             for d in range(1, LATS):
                 sems = ss4.at[h, u], rs4.at[h, u]
-                last.append(lat_send(s4[h].at[u], r4[h].at[u], *sems, d))
-                last[-1].start()
+                lat_send(s4[h].at[u], r4[h].at[u], *sems, d).start()
             r4[h][u, l] = s4[h][u, l]
 
     slot = lax.rem(lane_iota((fold, 128)), 64) // 16
     for u in range(2):
         for h in range(2):
-            for d in range(1, LATS):
-                sems = ss4.at[h, u], rs4.at[h, u]
-                lat_recv(s4[h].at[u], r4[h].at[u], *sems, d).wait_recv()
+            last_all(h, u).wait_recv()
         here = pl.ds(span * u, span)
         re, im = unpack_halves({
             (a, h): r4[h][u, a, : span // 2, :] for a in range(LATS) for h in range(2)
@@ -747,11 +741,12 @@
         out[0, here, :] = field[0] + even[0] + odd[0] - weight * carried[:, SIDE:]
         out[1, here, :] = field[1] + even[1] + odd[1] + weight * carried[:, :SIDE]
 
-    for copy in first[1] + last:
-        copy.wait_send()
+    first_all(1).wait_send()
     for h in range(2):
-        each(lambda d, h=h: to_rows(h, d).wait_send())
-    each(lambda d: to_columns(1, d).wait_send())
+        rows_all(h).wait_send()
+        for u in range(2):
+            last_all(h, u).wait_send()
+    columns_all(1).wait_send()
 
 
 def fused(light_field, lateral_phase, spectral_phase, occupation, bin_decay, bin_detune, group_bin):
@@ -759,9 +754,9 @@
     vmem, sems = pltpu.VMEM, pltpu.SemaphoreType.DMA
     exchange = [
         vmem((2, LATS, SIDE // 2, 128), F32), vmem((2, LATS, SIDE // 2, 128), F32),
-        vmem((2, LATS, SIDE // 2, 128), F32), vmem((2, TIMES, LATS, PART, 128), F32),
-        vmem((TIMES, LATS, PART + 8, 128), F32), vmem((LATS, TIMES, PART + 8, 128), F32),
-        vmem((TIMES, LATS, PART, 128), F32), vmem((LATS, TIMES, PART, 128), F32),
+        vmem((2, LATS, SIDE // 2, 128), F32), vmem((2, TOTAL, PART, 128), F32),
+        vmem((TOTAL, PART + 8, 128), F32), vmem((TOTAL, PART + 8, 128), F32),
+        vmem((TOTAL, PART, 128), F32), vmem((TOTAL, PART, 128), F32),
         vmem((2, LATS, 5 * SIDE // 16, 128), F32), vmem((2, LATS, 5 * SIDE // 16, 128), F32),
         vmem((2, LATS, SIDE // 4, 128), F32), vmem((2, LATS, SIDE // 4, 128), F32),
     ]
@@ -773,7 +768,7 @@
     fixed = constants()
     tables += [vmem(light_field.shape, F32), vmem(occupation.shape, F32)]
     tables += [vmem(c.shape, c.dtype) for c in fixed]
-    semaphores = [sems((2, LATS))] * 2 + [sems((2, TOTAL))] * 4 + [sems((2, 2, LATS))] * 2
+    semaphores = [sems((2,))] * 6 + [sems((2, 2))] * 2
     semaphores += [sems((2 + len(fixed),))]
     in_vmem, anywhere = pl.BlockSpec(memory_space=pltpu.VMEM), pl.BlockSpec(memory_space=pl.ANY)
     return pl.pallas_call(

time: 69.7 us -> 64.6 us (0.927)
  Pallas kernels: 65.3 us -> 60.2 us
    pallas_call x1, Pallas kernels: 65.3 us -> 60.2 us  [fused(): pl.pallas_call(kernel, out_shape=jax.ShapeDtypeStruct(light_field.shape,...]
where the time goes in v5:
time: 64.6 us; the launch traced here: 64.3 us
  Pallas kernels  60.2 us (93%)
  local copies, waits for them, and re-layouts  4.11 us (6%)
    pallas_call x1, Pallas kernels, fused(): pl.pallas_call(kernel, out_shape=jax.ShapeDtypeStruct(light_field.shape,...  60.2 us
    unnamed x5, local copies, waits for them, and re-layouts  2.56 us

profile of v5, /device:TPU:0, one launch (start us, length us, event | category | flops | bytes accessed | tf_op | source)
XLA Modules:
  0.0 64.3 jit_solution(4448834839915745967)
XLA Ops:
  0.0 0.0 copy-start.1
  0.0 0.7 %copy-done.1 = f32[1024]{0:T(1024)S(1)} copy-done((f32[1024]{0:T(1024)S(1)}, f32[1024]{0:T(1024)}, u32[]{:S(2)}) %copy-start.1) | copy-done | bytes 4120
  0.7 0.0 copy-start
  0.7 0.8 %reshape.6.latp = f32[256,4]{1,0:T(8,128)} reshape(f32[1024]{0:T(1024)S(1)} %copy-done.1) | data formatting | bytes 8192 | tf_op jit(solution)/shard_map/reshape | solution.py:785
  1.5 0.0 copy-done
  1.5 0.1 reshape.7
  1.6 0.7 %copy.12 = f32[256,8]{0,1:T(8,128)} copy(f32[256,8]{1,0:T(8,128)S(1)} %reshape.7) | data formatting | bytes 16384 | tf_op jit(solution)/shard_map/reshape | solution.py:786
  2.2 60.2 %shard_map.109 = f32[2,256,256]{2,1,0:T(8,128)} custom-call(f32[2,256,256]{2,1,0:T(8,128)} %lf_hbm.1, f32[256,4]{1,0:T(8,128)} %reshape.6.latp, f32[8,256]{1,0:T(8,128)} %bitcast.4, f32[128,256]{1,0:T(8,128)} %occ_hbm.1, f32[1,32]{1,0:T(1,128)} %bitcast.5, f32[1,32]{1,0:T(1,128)} %bitcast.6, s32[1,128]{1,0:T(1,128)} %bitcast.7, ...), custom_call_target="tpu_custom_call" | custom-call | tf_op jit(solution)/shard_map/pallas_call | solution.py:774
  62.5 1.9 %copy.14 = f32[2,256,256]{2,1,0:T(8,128)} copy(f32[2,256,256]{2,1,0:T(8,128)} %shard_map.109) | data formatting | bytes 1048576
Async XLA Ops:
  0.0 0.7 %copy-start.1 = (f32[1024]{0:T(1024)S(1)}, f32[1024]{0:T(1024)}, u32[]{:S(2)}) copy-start(f32[1024]{0:T(1024)} %param.12) | copy-start | bytes 12292
  0.7 0.8 %copy-start = (f32[2048]{0:T(1024)S(1)}, f32[2048]{0:T(1024)}, u32[]{:S(2)}) copy-start(f32[2048]{0:T(1024)} %param.13) | copy-start | bytes 24580

commit v6 on v5

--- a/solution.py
+++ b/solution.py
@@ -245,7 +245,9 @@
 
 
 def dot3(a, b):
-    return dot(a[0], b[0]) + dot(a[1], b[0]) + dot(a[0], b[1])
+    return dot(
+        jnp.concatenate([a[0], a[1], a[0]], axis=1), jnp.concatenate([b[0], b[0], b[1]], axis=0)
+    )
 
 
 def cmul(a, b):
@@ -348,11 +350,11 @@
 
 def kernel(
     lf_hbm, latp, specp, occ_hbm, dec_ref, det_ref, gb_ref, wh_hbm, wl_hbm, rows_hbm, cols_hbm,
-    out,
-    s1, r1, s2, r2, s3a, r3a, s3b, r3b, s4a, r4a, s4b, r4b,
+    out_hbm,
+    out, s1, r1, s2, r2, s3a, r3a, s3b, r3b, s4a, r4a, s4b, r4b,
     tw_c, tw_s, th_c, th_s, ph_c, ph_s, ct, q_hi, q_lo, p_hi, p_lo, kev, kod, kfe, kfo, spec,
     lf, occ, wh, wl, rows_ref, cols_ref,
-    ss1, rs1, ss2, rs2, ss3, rs3, ss4, rs4, load_sem,
+    ss1, rs1, ss2, rs2, ss3, rs3, ss4, rs4, load_sem, store_sem,
 ):
     loads = []
     for i, (src, dst) in enumerate((
@@ -435,14 +437,25 @@
     group = lax.rem(lane_iota(whole), 64) // 16
     sign = jnp.where(lane_iota(whole) < 64, -1.0, 1.0)
     phase = latp[...]
-    turn_c, turn_s = jnp.cos(phase) * (1.0 / WIDE), jnp.sin(phase) * (1.0 / WIDE)
+    turns = jnp.cos(phase) * (1.0 / WIDE), jnp.sin(phase) * (1.0 / WIDE)
+    per_row = 128 // LATS
+    chosen = lane_iota((per_row, 128))
+    chosen = chosen - LATS * lax.broadcasted_iota(jnp.int32, (per_row, 128), 0)
+
+    def spread_out(table, k):
+        rows = []
+        for i in range(WIDE // 128):
+            one = jnp.where(chosen == k, table[i : i + 1], 0.0)
+            rows.append(jnp.broadcast_to(jnp.sum(one, axis=1, keepdims=True), (per_row, 128)))
+        return jnp.concatenate(rows, axis=0)
+
     second_set = lax.rem(lane_part((SIDE // 2, 128)), 2) == 1
     second_key = lax.rem(lane_part(whole), 2) == 1
     for k in range(LATS):
         tw_c[k] = jnp.broadcast_to(cols_ref[:, k : k + 1], whole)
         tw_s[k] = jnp.broadcast_to(cols_ref[:, LATS + k : LATS + k + 1], whole) * sign
-        ph_c[k] = jnp.broadcast_to(turn_c[:, k : k + 1], whole)
-        ph_s[k] = jnp.broadcast_to(turn_s[:, k : k + 1], whole) * sign
+        ph_c[k] = spread_out(turns[0], k)
+        ph_s[k] = spread_out(turns[1], k) * sign
         for full, parted in ((tw_c, th_c), (tw_s, th_s)):
             one, two = part_rows(full[k])
             parted[k] = jnp.where(second_set, two, one)
@@ -557,8 +570,9 @@
 
     loads[4].wait()
     loads[5].wait()
-    spec[0] = jnp.cos(specp[...]) * (1.0 / LONG)
-    spec[1] = jnp.sin(specp[...]) * (1.0 / LONG)
+    phase = specp[...].T
+    spec[0] = jnp.cos(phase) * (1.0 / LONG)
+    spec[1] = jnp.sin(phase) * (1.0 / LONG)
 
     dec_row, det_row = dec_ref[...], det_ref[...]
     square = (BIN_COUNT, BIN_COUNT)
@@ -716,6 +730,7 @@
                 lat_send(s4[h].at[u], r4[h].at[u], *sems, d).start()
             r4[h][u, l] = s4[h][u, l]
 
+    stores = []
     slot = lax.rem(lane_iota((fold, 128)), 64) // 16
     for u in range(2):
         for h in range(2):
@@ -740,6 +755,10 @@
         odd = cmul(odd, conj(t2))
         out[0, here, :] = field[0] + even[0] + odd[0] - weight * carried[:, SIDE:]
         out[1, here, :] = field[1] + even[1] + odd[1] + weight * carried[:, :SIDE]
+        stores.append(
+            pltpu.make_async_copy(out.at[:, here], out_hbm.at[:, here], store_sem.at[u])
+        )
+        stores[-1].start()
 
     first_all(1).wait_send()
     for h in range(2):
@@ -747,12 +766,15 @@
         for u in range(2):
             last_all(h, u).wait_send()
     columns_all(1).wait_send()
+    for copy in stores:
+        copy.wait()
 
 
 def fused(light_field, lateral_phase, spectral_phase, occupation, bin_decay, bin_detune, group_bin):
     tile = (SIDE, 128)
     vmem, sems = pltpu.VMEM, pltpu.SemaphoreType.DMA
     exchange = [
+        vmem(light_field.shape, F32),
         vmem((2, LATS, SIDE // 2, 128), F32), vmem((2, LATS, SIDE // 2, 128), F32),
         vmem((2, LATS, SIDE // 2, 128), F32), vmem((2, TOTAL, PART, 128), F32),
         vmem((TOTAL, PART + 8, 128), F32), vmem((TOTAL, PART + 8, 128), F32),
@@ -769,21 +791,21 @@
     tables += [vmem(light_field.shape, F32), vmem(occupation.shape, F32)]
     tables += [vmem(c.shape, c.dtype) for c in fixed]
     semaphores = [sems((2,))] * 6 + [sems((2, 2))] * 2
-    semaphores += [sems((2 + len(fixed),))]
+    semaphores += [sems((2 + len(fixed),)), sems((2,))]
     in_vmem, anywhere = pl.BlockSpec(memory_space=pltpu.VMEM), pl.BlockSpec(memory_space=pl.ANY)
     return pl.pallas_call(
         kernel,
         out_shape=jax.ShapeDtypeStruct(light_field.shape, F32),
         in_specs=[anywhere] + [in_vmem] * 2 + [anywhere] + [in_vmem] * 3 + [anywhere] * len(fixed),
-        out_specs=pl.BlockSpec(memory_space=pltpu.VMEM),
+        out_specs=anywhere,
         scratch_shapes=exchange + tables + semaphores,
         compiler_params=pltpu.CompilerParams(
             collective_id=0, has_side_effects=True, vmem_limit_bytes=56 * 1024 * 1024
         ),
     )(
         light_field,
-        lateral_phase.reshape(SIDE, LATS),
-        spectral_phase.reshape(SIDE, TIMES).T,
+        lateral_phase.reshape(WIDE // 128, 128),
+        spectral_phase.reshape(SIDE, TIMES),
         occupation,
         bin_decay[None],
         bin_detune[None],

time: 64.6 us -> 63.5 us (0.983)
  local copies, waits for them, and re-layouts: 4.11 us -> 3.32 us
    reshape x1 -> x0, local copies, waits for them, and re-layouts: 0.79 us -> none  [fused(): lateral_phase.reshape(SIDE, LATS)]
    reshape x2 -> x1, local copies, waits for them, and re-layouts: 0.76 us -> 1.45 us  [fused(): spectral_phase.reshape(SIDE, TIMES)]
    unnamed x5 -> x1, local copies, waits for them, and re-layouts: 2.56 us -> 1.87 us
where the time goes in v6:
time: 63.5 us; the launch traced here: 63.3 us
  Pallas kernels  59.9 us (94%)
  local copies, waits for them, and re-layouts  3.32 us (5%)
    pallas_call x1, Pallas kernels, fused(): pl.pallas_call(kernel, out_shape=jax.ShapeDtypeStruct(light_field.shape,...  59.9 us
    unnamed x1, local copies, waits for them, and re-layouts  1.87 us
    reshape x1, local copies, waits for them, and re-layouts, fused(): spectral_phase.reshape(SIDE, TIMES)  1.45 us

profile of v6, /device:TPU:0, one launch (start us, length us, event | category | flops | bytes accessed | tf_op | source)
XLA Modules:
  0.0 63.3 jit_solution(11469351007884582096)
XLA Ops:
  0.0 1.5 %reshape.7.specp = f32[256,8]{1,0:T(8,128)} reshape(f32[2048]{0:T(1024)} %param.13) | data formatting | bytes 16384 | tf_op jit(solution)/shard_map/reshape | solution.py:808
  1.5 59.9 %shard_map.109 = f32[2,256,256]{2,1,0:T(8,128)} custom-call(f32[2,256,256]{2,1,0:T(8,128)} %lf_hbm.1, f32[8,128]{1,0:T(8,128)} %bitcast.4, f32[256,8]{1,0:T(8,128)} %reshape.7.specp, f32[128,256]{1,0:T(8,128)} %occ_hbm.1, f32[1,32]{1,0:T(1,128)} %bitcast.5, f32[1,32]{1,0:T(1,128)} %bitcast.6, s32[1,128]{1,0:T(1,128)} %bitcast.7, ...), custom_call_target="tpu_custom_call" | custom-call | tf_op jit(solution)/shard_map/pallas_call | solution.py:796
  61.4 1.9 %copy.13 = f32[2,256,256]{2,1,0:T(8,128)} copy(f32[2,256,256]{2,1,0:T(8,128)} %shard_map.109) | data formatting | bytes 1048576

commit v7 on v6

--- a/solution.py
+++ b/solution.py
@@ -351,7 +351,7 @@
 def kernel(
     lf_hbm, latp, specp, occ_hbm, dec_ref, det_ref, gb_ref, wh_hbm, wl_hbm, rows_hbm, cols_hbm,
     out_hbm,
-    out, s1, r1, s2, r2, s3a, r3a, s3b, r3b, s4a, r4a, s4b, r4b,
+    out, s1, r1, s2, r2, s3a, r3a, s3b, r3b, s3c, r3c, s3d, r3d, s4a, r4a, s4b, r4b,
     tw_c, tw_s, th_c, th_s, ph_c, ph_s, ct, q_hi, q_lo, p_hi, p_lo, kev, kod, kfe, kfo, spec,
     lf, occ, wh, wl, rows_ref, cols_ref,
     ss1, rs1, ss2, rs2, ss3, rs3, ss4, rs4, load_sem, store_sem,
@@ -403,21 +403,21 @@
         part = ref.at[pl.ds(0, count)]
         return remote(part, part, ss, rs, lats[1], m)
 
-    s3, r3 = (s3a, s3b), (r3a, r3b)
+    s3, r3 = ((s3a, s3b), (s3c, s3d)), ((r3a, r3b), (r3c, r3d))
 
     def to_rows(h, tl, tm):
         src = s2.at[h, tl, pl.ds(pl.multiple_of(tm * PART, PART), PART)]
         return remote(src, r2.at[h, m * LATS + l], ss2.at[h], rs2.at[h], tl, tm)
 
-    def to_columns(h, tl, tm):
-        dst = r3[h].at[l * TIMES + m]
-        return remote(s3[h].at[tm * LATS + tl], dst, ss3.at[h], rs3.at[h], tl, tm)
+    def to_columns(v, h, tl, tm):
+        dst = r3[v][h].at[l * TIMES + m]
+        return remote(s3[v][h].at[tm * LATS + tl], dst, ss3.at[v, h], rs3.at[v, h], tl, tm)
 
     def rows_all(h):
         return all_of(r2.at[h], TOTAL - 1, ss2.at[h], rs2.at[h])
 
-    def columns_all(h):
-        return all_of(r3[h], TOTAL - 1, ss3.at[h], rs3.at[h])
+    def columns_all(v, h):
+        return all_of(r3[v][h], TOTAL - 1, ss3.at[v, h], rs3.at[v, h])
 
     loads[0].wait()
     for (t, h), tile in pack_halves(part_rows(lf[0]), part_rows(lf[1])).items():
@@ -475,7 +475,8 @@
         return tuple(jnp.concatenate([item[c] for item in items], axis=0) for c in (0, 1))
 
     def unstack(value):
-        return [tuple(v[ROWS * k : ROWS * (k + 1)] for v in value) for k in range(TIMES)]
+        size = value[0].shape[0] // TIMES
+        return [tuple(v[size * k : size * (k + 1)] for v in value) for k in range(TIMES)]
 
     def time_dft(items):
         items = small_fft(items, -1)
@@ -646,44 +647,60 @@
 
     for h in range(2):
         rows_all(h).wait_recv()
-    field = []
-    for k in range(TIMES):
-        re, im = unpack_halves({(a, h): r2[h, k * LATS + a] for a in range(LATS) for h in range(2)})
-        field.append((jnp.concatenate(re, axis=0), jnp.concatenate(im, axis=0)))
+    step = power(float(SIDE), step_dec, step_det)
+    slot = lax.rem(lane_iota((8, SIDE)) // 16, 4)
     turn_row = stack([
-        tuple(jnp.broadcast_to(spec[c, k : k + 1, :], (ROWS, SIDE)) for c in (0, 1))
+        tuple(jnp.broadcast_to(spec[c, k : k + 1, :], (PART, SIDE)) for c in (0, 1))
         for k in range(TIMES)
     ])
-    once = cmul(time_dft(field), turn_row)
-    twisted = time_dft(twist(time_inverse_dft(once), False))
-    twisted = time_inverse_dft(cmul(twisted, (kod[0], kod[1])))
-    late = time_dft(twist(twisted, True))
-    straight = cmul(once, (kev[0], kev[1]))
-    once = cmul((straight[0] + late[0], straight[1] + late[1]), turn_row)
-    field = time_inverse_dft(once)
-    flat = stack(field)
-    ends = dot3(halves(jnp.concatenate(flat, axis=1)), (p_hi[...], p_lo[...]))
-    ends = unstack((ends[:, :SIDE], ends[:, SIDE:]))
-    step = power(float(SIDE), step_dec, step_det)
-    slot = lax.rem(lane_iota((8, SIDE)) // 16, 4)
-    state = (jnp.zeros((ROWS, SIDE), F32), jnp.zeros((ROWS, SIDE), F32))
+
+    def half_of(table, v):
+        picked = []
+        for c in (0, 1):
+            x = table[c].reshape(TIMES, 2, 2, 8, SIDE)[:, :, v]
+            picked.append(x.reshape(SIDE // 2, SIDE))
+        return tuple(picked)
+
+    folded = [[jnp.zeros((8, SIDE), F32) for c in (0, 1)] for k in range(TIMES)]
+    for v in range(2):
+        rows = slice(8 * v, 8 * v + 8)
+        field = []
+        for k in range(TIMES):
+            tiles = {(a, h): r2[h, k * LATS + a, rows] for a in range(LATS) for h in range(2)}
+            re, im = unpack_halves(tiles)
+            field.append((jnp.concatenate(re, axis=0), jnp.concatenate(im, axis=0)))
+        once = cmul(time_dft(field), turn_row)
+        twisted = time_dft(twist(time_inverse_dft(once), False))
+        twisted = time_inverse_dft(cmul(twisted, half_of(kod, v)))
+        late = time_dft(twist(twisted, True))
+        straight = cmul(once, half_of(kev, v))
+        once = cmul((straight[0] + late[0], straight[1] + late[1]), turn_row)
+        field = time_inverse_dft(once)
+        for k in range(TIMES):
+            re, im = ((x[:8], x[8:]) for x in field[k])
+            for (a, h), tile in pack_halves(re, im).items():
+                s3[v][h][k * LATS + a, :8, :] = tile
+        if v == 0:
+            for h in range(2):
+                each(lambda tl, tm, h=h: to_columns(0, h, tl, tm).start())
+        flat = stack(field)
+        ends = dot3(halves(jnp.concatenate(flat, axis=1)), (p_hi[...], p_lo[...]))
+        ends = unstack((ends[:, :SIDE], ends[:, SIDE:]))
+        state = (jnp.zeros((PART, SIDE), F32), jnp.zeros((PART, SIDE), F32))
+        for k in range(TIMES):
+            for c in (0, 1):
+                for g in range(2):
+                    piece = state[c][8 * g : 8 * g + 8]
+                    folded[k][c] = jnp.where(slot == 2 * g + v, piece, folded[k][c])
+            moved = cmul(state, step)
+            state = (moved[0] + ends[k][0], moved[1] + ends[k][1])
     for k in range(TIMES):
-        folded = []
-        for c in (0, 1):
-            total = state[c][:8]
-            for g in range(1, 4):
-                total = jnp.where(slot == g, state[c][8 * g : 8 * g + 8], total)
-            folded.append(total)
-        for a, tile in enumerate(pack(*folded)):
-            s3a[k * LATS + a, PART:, :] = tile
-        moved = cmul(state, step)
-        state = (moved[0] + ends[k][0], moved[1] + ends[k][1])
-        re, im = ((v[:PART], v[PART:]) for v in field[k])
-        for (a, h), tile in pack_halves(re, im).items():
-            s3[h][k * LATS + a, :PART, :] = tile
-    each(lambda tl, tm: to_columns(0, tl, tm).start())
-    for h in range(2):
-        r3[h][l * TIMES + m] = s3[h][m * LATS + l]
+        for a, tile in enumerate(pack(*folded[k])):
+            s3c[k * LATS + a, 8:, :] = tile
+    each(lambda tl, tm: to_columns(1, 0, tl, tm).start())
+    for v in range(2):
+        for h in range(2):
+            r3[v][h][l * TIMES + m] = s3[v][h][m * LATS + l]
 
     t2 = rows_ref[0, 2 * TIMES : 2 * TIMES + 1, :], rows_ref[1, 2 * TIMES : 2 * TIMES + 1, :]
     q = (q_hi[...], q_lo[...])
@@ -694,8 +711,8 @@
     kfe[0], kfe[1] = -gain * even[1], gain * even[0]
     kfo[0], kfo[1] = -gain * odd[1], gain * odd[0]
 
-    columns_all(0).wait_send()
-    each(lambda tl, tm: to_columns(1, tl, tm).start())
+    columns_all(1, 0).wait_send()
+    each(lambda tl, tm: to_columns(1, 1, tl, tm).start())
     span = SIDE // 2
     fold = span // 8
     slot = lax.rem(lane_iota((fold, 128)), 64) // 8
@@ -705,13 +722,15 @@
         return all_of(r4[h].at[u], LATS - 1, ss4.at[h, u], rs4.at[h, u])
 
     for h in range(2):
-        columns_all(h).wait_recv()
+        columns_all(0, h).wait_recv()
+        columns_all(1, h).wait_recv()
         tiles, states = [], []
         for a in range(LATS):
             mine = slice(a * TIMES, (a + 1) * TIMES)
-            tiles.append(r3[h][mine, :PART, :].reshape(span, 128))
+            both = jnp.stack([r3[v][h][mine, :8, :] for v in range(2)], axis=1)
+            tiles.append(both.reshape(span, 128))
             if h == 0:
-                extra = r3a[mine, PART:, :].reshape(8 * TIMES, 128)
+                extra = r3c[mine, 8:, :].reshape(8 * TIMES, 128)
                 extra = [roll(extra, -16 * g).reshape(TIMES, 8, 128) for g in range(4)]
                 states.append(jnp.stack(extra, axis=1).reshape(SIDE, 128))
         spectrum = lateral_spectrum(tiles, states)
@@ -765,7 +784,8 @@
         rows_all(h).wait_send()
         for u in range(2):
             last_all(h, u).wait_send()
-    columns_all(1).wait_send()
+    for v, h in ((0, 0), (0, 1), (1, 1)):
+        columns_all(v, h).wait_send()
     for copy in stores:
         copy.wait()
 
@@ -777,8 +797,7 @@
         vmem(light_field.shape, F32),
         vmem((2, LATS, SIDE // 2, 128), F32), vmem((2, LATS, SIDE // 2, 128), F32),
         vmem((2, LATS, SIDE // 2, 128), F32), vmem((2, TOTAL, PART, 128), F32),
-        vmem((TOTAL, PART + 8, 128), F32), vmem((TOTAL, PART + 8, 128), F32),
-        vmem((TOTAL, PART, 128), F32), vmem((TOTAL, PART, 128), F32),
+        *[vmem((TOTAL, rows, 128), F32) for rows in (8, 8, 8, 8, 16, 16, 8, 8)],
         vmem((2, LATS, 5 * SIDE // 16, 128), F32), vmem((2, LATS, 5 * SIDE // 16, 128), F32),
         vmem((2, LATS, SIDE // 4, 128), F32), vmem((2, LATS, SIDE // 4, 128), F32),
     ]
@@ -790,7 +809,7 @@
     fixed = constants()
     tables += [vmem(light_field.shape, F32), vmem(occupation.shape, F32)]
     tables += [vmem(c.shape, c.dtype) for c in fixed]
-    semaphores = [sems((2,))] * 6 + [sems((2, 2))] * 2
+    semaphores = [sems((2,))] * 4 + [sems((2, 2))] * 4
     semaphores += [sems((2 + len(fixed),)), sems((2,))]
     in_vmem, anywhere = pl.BlockSpec(memory_space=pltpu.VMEM), pl.BlockSpec(memory_space=pl.ANY)
     return pl.pallas_call(

time: 63.5 us -> 63.3 us (level)
  no operation moved by 1% of the time
where the time goes in v7:
time: 63.3 us; the launch traced here: 63 us
  Pallas kernels  59.7 us (94%)
  local copies, waits for them, and re-layouts  3.32 us (5%)
    pallas_call x1, Pallas kernels, fused(): pl.pallas_call(kernel, out_shape=jax.ShapeDtypeStruct(light_field.shape,...  59.7 us
    unnamed x1, local copies, waits for them, and re-layouts  1.87 us
    reshape x1, local copies, waits for them, and re-layouts, fused(): spectral_phase.reshape(SIDE, TIMES)  1.45 us

profile of v7, /device:TPU:0, one launch (start us, length us, event | category | flops | bytes accessed | tf_op | source)
XLA Modules:
  0.0 63.0 jit_solution(10283743155233434857)
XLA Ops:
  0.0 1.5 %reshape.7.specp = f32[256,8]{1,0:T(8,128)} reshape(f32[2048]{0:T(1024)} %param.13) | data formatting | bytes 16384 | tf_op jit(solution)/shard_map/reshape | solution.py:827
  1.5 59.7 %shard_map.109 = f32[2,256,256]{2,1,0:T(8,128)} custom-call(f32[2,256,256]{2,1,0:T(8,128)} %lf_hbm.1, f32[8,128]{1,0:T(8,128)} %bitcast.4, f32[256,8]{1,0:T(8,128)} %reshape.7.specp, f32[128,256]{1,0:T(8,128)} %occ_hbm.1, f32[1,32]{1,0:T(1,128)} %bitcast.5, f32[1,32]{1,0:T(1,128)} %bitcast.6, s32[1,128]{1,0:T(1,128)} %bitcast.7, ...), custom_call_target="tpu_custom_call" | custom-call | tf_op jit(solution)/shard_map/pallas_call | solution.py:815
  61.2 1.9 %copy.13 = f32[2,256,256]{2,1,0:T(8,128)} copy(f32[2,256,256]{2,1,0:T(8,128)} %shard_map.109) | data formatting | bytes 1048576
